TPU v7x, 128 devices: a whole 4x4x4 slice. The times are simulated.
128 devices in a mesh: ep: 32 (over y, x, core), head: 4 (over z).
Axes of the slice: x: 4, y: 4, z: 4, core: 2. Of those that a mesh axis runs over, the one named last changes fastest.
Arguments:
- queries: bfloat16 [256, 128, 576], P('ep', 'head'), may hold values from -60 to 60
- latent_cache: bfloat16 [256, 1024, 576], P('ep'), may hold values from -6 to 6
- lengths: int32 [256], P('ep'), may hold values from 2 to 1024, as said below
- value_up: bfloat16 [128, 512, 128], P('head'), may hold values from -1 to 1
- output_weight: bfloat16 [16384, 7168], P('head', 'ep'), may hold values from -0.046875 to 0.046875
- residual: bfloat16 [256, 7168], P(None, 'ep'), may hold values from -6 to 6
- norm_gain: float32 [7168], P('ep'), may hold values from 0.1 to 1.9
- expert_ids: int32 [256, 8], replicated, may hold values from 0 to 31, all different within a row; in each aligned block of 256 rows (0 to 255, 256 to 511, ...) at most 128 rows name the same one
- expert_weight: float32 [256, 8], replicated, may hold values from 0.2 to 1
- gate_weight: bfloat16 [32, 7168, 1024], P('ep', None, 'head'), may hold values from -0.0625 to 0.0625
- up_weight: bfloat16 [32, 7168, 1024], P('ep', None, 'head'), may hold values from -0.0625 to 0.0625
- down_weight: bfloat16 [32, 1024, 7168], P('ep', 'head'), may hold values from -0.25 to 0.25
Outputs:
- mixed: bfloat16 [256, 7168], P(None, 'ep')
Inputs may be any that keep to these rules, and one draw needn't show every extreme that they name: Every sequence's cache holds valid rows at positions 0 to lengths - 1; some sequence has a full cache of 1024 positions. `expert_ids`: no expert is chosen by more than 128 tokens; some expert is chosen by exactly 128. The experts of one token differ.
All inputs are finite; a program needn't handle non-finite values.
Results may differ from a plain program's by a relative error of at most 0.013.
Values may be sent and summed in bfloat16 or wider, within the bound.
No kernel may reach another device: no remote copies, remote signals or barrier semaphores. Data moves between devices by JAX's collectives and lax.ppermute only.
A program may use at most 128 MiB of HBM per device.

v0:
```python
import jax
import jax.numpy as jnp
from jax import lax
from jax.sharding import PartitionSpec as P

D = 7168


SCORE_SCALE = 192.0 ** (-0.5)
NORM_EPS = 1e-06


def routing_slots(expert_ids, experts, capacity):
    flat_ids = expert_ids.reshape(-1)
    onehot = (flat_ids[:, None] == jnp.arange(experts, dtype=jnp.int32)[None, :]).astype(jnp.int32)
    slot_rank = jnp.sum((jnp.cumsum(onehot, axis=0) - 1) * onehot, axis=1)
    destination = flat_ids * capacity + slot_rank
    owners = jnp.arange(flat_ids.shape[0], dtype=jnp.int32) // expert_ids.shape[1]
    slot_owner = jnp.zeros((experts * capacity,), jnp.int32).at[destination].set(owners)
    filled = jnp.zeros((experts * capacity,), jnp.bool_).at[destination].set(True)
    return (destination, slot_rank, slot_owner, filled)


def per_device(
    queries,
    latent_cache,
    lengths,
    value_up,
    output_weight,
    residual,
    norm_gain,
    expert_ids,
    expert_weight,
    gate_weight,
    up_weight,
    down_weight,
):
    local_seqs = queries.shape[0]
    positions = jnp.arange(latent_cache.shape[1], dtype=jnp.int32)
    scores = (
        jnp.einsum("shd,scd->shc", queries, latent_cache, preferred_element_type=jnp.float32)
        * SCORE_SCALE
    )
    allowed = (positions[None, :] < lengths[:, None])[:, None, :]
    scores = jnp.where(allowed, scores, jnp.float32(-1e30))
    row_peaks = jnp.max(scores, axis=2, keepdims=True)
    exponents = jnp.exp(scores - row_peaks)
    attn_weights = (exponents / jnp.sum(exponents, axis=2, keepdims=True)).astype(jnp.bfloat16)
    latent_width = value_up.shape[1]
    contexts = jnp.einsum(
        "shc,scl->shl",
        attn_weights,
        latent_cache[:, :, :latent_width],
        preferred_element_type=jnp.float32,
    ).astype(jnp.bfloat16)
    values = jnp.einsum("shl,hlv->shv", contexts, value_up, preferred_element_type=jnp.float32)
    values = values.astype(jnp.bfloat16).reshape(local_seqs, -1)
    partial_attn = jnp.dot(
        lax.all_gather(values, "ep", axis=0, tiled=True),
        output_weight,
        preferred_element_type=jnp.float32,
    )
    attention = lax.psum(partial_attn, "head")
    stream = residual.astype(jnp.float32) + attention
    squares = lax.psum(jnp.sum(stream * stream, axis=1), "ep")
    normed = (stream * lax.rsqrt(squares / D + NORM_EPS)[:, None] * norm_gain[None, :]).astype(
        jnp.bfloat16
    )
    experts = lax.axis_size("ep")
    top_count = expert_ids.shape[1]
    capacity = min(2 * local_seqs * top_count, local_seqs * experts)
    column_width = normed.shape[1]
    destination, slot_rank, slot_owner, filled = routing_slots(expert_ids, experts, capacity)
    slot_table = slot_owner.reshape(experts, capacity).T
    slot_filled = filled.reshape(experts, capacity).T
    zero_value = jnp.zeros((), jnp.bfloat16)
    outgoing = jnp.where(slot_filled[:, :, None], normed[slot_table], zero_value)
    outgoing = outgoing.reshape(capacity, experts * column_width)
    arrived = lax.all_to_all(outgoing, "ep", split_axis=1, concat_axis=1, tiled=True)
    gate_out = jnp.dot(arrived, gate_weight[0], preferred_element_type=jnp.float32)
    up_out = jnp.dot(arrived, up_weight[0], preferred_element_type=jnp.float32)
    hidden_units = (jax.nn.silu(gate_out) * up_out).astype(jnp.bfloat16)
    summed = lax.psum(
        jnp.dot(hidden_units, down_weight[0], preferred_element_type=jnp.float32), "head"
    ).astype(jnp.bfloat16)
    returned = lax.all_to_all(summed, "ep", split_axis=1, concat_axis=0, tiled=True)
    picked = returned[destination].astype(jnp.float32).reshape(-1, top_count, column_width)
    combined = jnp.sum(picked * expert_weight[:, :, None], axis=1)
    return (stream + combined).astype(jnp.bfloat16)


def solution(mesh):
    placed = (
        P("ep", "head", None),
        P("ep", None, None),
        P("ep"),
        P("head", None, None),
        P("head", "ep"),
        P(None, "ep"),
        P("ep"),
        P(),
        P(),
        P("ep", None, "head"),
        P("ep", None, "head"),
        P("ep", "head", None),
    )
    return jax.shard_map(
        per_device, mesh=mesh, in_specs=placed, out_specs=P(None, "ep"), check_vma=False
    )
```

profile of v0, /device:TPU:1, one launch (start us, length us, event | category | flops | bytes accessed | tf_op | source)
XLA Modules:
  0.0 368.8 jit_solution(1116848977464259477)
XLA Ops:
  7.4 5.5 %fusion.12 = f32[8,32,1024]{2,1,0:T(8,128)S(1)} fusion(bf16[8,32,576]{2,1,0:T(8,128)(2,1)} %param.12, bf16[8,1024,576]{1,2,0:T(8,128)(2,1)} %param.13, pred[8,1024]{1,0:T(8,128)(4,1)S(1)} %iota_compare_fusion.2), kind=kOutput, calls=%fused_computation.19 | convolution fusion | flops 302514176 | bytes 10788864 | tf_op jit(solution)/shard_map/shd,scd->shc/dot_general | solution.py:41
  13.2 6.0 %fusion.13 = bf16[8,32,512]{2,1,0:T(8,128)(2,1)S(1)} fusion(bf16[8,1024,576]{1,2,0:T(8,128)(2,1)} %param.13, f32[8,32]{1,0:T(8,128)S(1)} %fusion.45, f32[8,32,1024]{2,1,0:T(8,128)S(1)} %fusion.12), kind=kOutput, calls=%fused_computation.20 | convolution fusion | flops 269354240 | bytes 10752000 | tf_op jit(solution)/shard_map/shc,scl->shl/dot_general | solution.py:50
  19.3 3.6 fusion.22
  23.3 9.1 %reduce-window.6 = s32[32,16,128]{2,1,0:T(8,128)S(1)} reduce-window(s32[32,16,128]{2,1,0:T(8,128)S(1)} %fusion.29, s32[]{:T(128)} %constant.44.clone.1), window={size=1x1x128 pad=0_0x0_0x127_0}, to_apply=%region_3.4 | reduce-window | flops 8323072 | bytes 524292 | tf_op jit(solution)/shard_map/reduce-window
  33.5 8.1 %scatter_custom_fusion.1 = s32[4096]{0:T(1024)S(1)} fusion(s32[2048]{0:T(1024)S(1)} %bitcast.70, s32[2048]{0:T(1024)S(1)} %add_select_fusion, s32[]{:T(128)} %constant.44.clone.1), kind=kCustom, calls=%fused_computation.55 | custom fusion | bytes 16388 | tf_op jit(solution)/shard_map/scatter | solution.py:19
  41.6 28.8 %all-gather.2.cloned.1.call-done = bf16[256,4096]{1,0:T(8,128)(2,1)} async-done(((bf16[8,4096]{1,0:T(8,128)(2,1)}), bf16[256,4096]{1,0:T(8,128)(2,1)}) %all-gather.2.cloned.1.call-update) | async-done | bytes 2097168 | tf_op jit(solution)/shard_map/all_gather | solution.py:59
  70.4 3.1 fusion.46
  73.7 9.1 %scatter_custom_fusion = pred[4096]{0:T(1024)(128)(4,1)S(1)} fusion(s32[2048]{0:T(1024)S(1)} %bitcast.71, pred[2048]{0:T(1024)(128)(4,1)S(1)} %broadcast.89, pred[]{:T(512)} %constant.17.clone.1), kind=kCustom, calls=%fused_computation.58 | custom fusion | bytes 4097 | tf_op jit(solution)/shard_map/scatter | solution.py:20
  82.8 29.3 %all-reduce.3.cloned.1.call-done = f32[256,224]{0,1:T(8,128)} async-done(((f32[256,224]{0,1:T(8,128)}), f32[256,224]{0,1:T(8,128)}) %all-reduce.3.cloned.1.call-update) | async-done | bytes 229392 | tf_op jit(solution)/shard_map/psum | solution.py:63
  113.1 65.0 %psum.22 = f32[256]{0:T(256)S(1)} all-reduce(f32[256]{0:T(256)S(1)} %multiply_reduce_fusion), channel_id=1, replica_groups=mesh['ep'=32,'head'=4] {'ep'}, use_global_device_ids=true, to_apply=%region_8.9 | all-reduce | flops 256 | bytes 2048 | tf_op jit(solution)/shard_map/psum | solution.py:65
  178.1 1.0 multiply_convert_fusion
  179.3 16.9 %gather_fusion = bf16[4096,224]{1,0:T(8,128)(2,1)} fusion(bf16[256,224]{1,0:T(8,128)(2,1)S(1)} %copy.47, s32[4096]{0:T(1024)S(1)} %broadcast_clamp_fusion), kind=kCustom, calls=%fused_computation | custom fusion | bytes 3686400 | tf_op jit(solution)/shard_map/gather | solution.py:77
  196.2 4.5 %copy.48 = bf16[128,32,224]{0,2,1:T(8,128)(2,1)} copy(bf16[128,32,224]{2,1,0:T(8,128)(2,1)} %bitcast.64) | data formatting | bytes 3670016 | tf_op jit(solution)/shard_map/gather | solution.py:77
  200.7 1.6 broadcast_select_fusion
  202.3 31.3 %all_to_all.28 = bf16[128,32,224]{0,2,1:T(8,128)(2,1)S(1)} all-to-all(bf16[128,32,224]{0,2,1:T(8,128)(2,1)S(1)} %broadcast_select_fusion), channel_id=1, replica_groups=mesh['ep'=32,'head'=4] {'ep'}, dimensions={1} | all-to-all | bytes 3670016 | tf_op jit(solution)/shard_map/all_to_all | solution.py:79
  233.7 1.3 copy-done.1
  235.7 7.7 %fusion.3 = f32[128,7168]{1,0:T(8,128)} fusion(bf16[1,256,7168]{2,1,0:T(8,128)(2,1)} %param.23, bf16[128,7168]{0,1:T(8,128)(2,1)} %bitcast.63, bf16[1,7168,256]{2,1,0:T(8,128)(2,1)} %param.22, f32[128,256]{1,0:T(8,128)S(1)} %fusion.7), kind=kOutput, calls=%fused_computation.7 | convolution fusion | flops 939720704 | bytes 12976128 | tf_op jit(solution)/shard_map/dot_general | solution.py:84
  243.4 67.9 %all-reduce.4 = bf16[128,7168]{1,0:T(8,128)(2,1)} all-reduce(f32[128,7168]{1,0:T(8,128)} %fusion.3), channel_id=1, replica_groups=mesh['ep'=32,'head'=4] {'head'}, use_global_device_ids=true, to_apply=%region_10.11 | all-reduce | flops 917504 | bytes 5505024 | tf_op jit(solution)/shard_map/psum | solution.py:83
  311.3 3.9 %copy.49 = bf16[128,7168]{0,1:T(8,128)(2,1)} copy(bf16[128,7168]{1,0:T(8,128)(2,1)} %all-reduce.4) | data formatting | bytes 3670016 | tf_op jit(solution)/shard_map/convert_element_type | solution.py:85
  315.2 6.9 %all-to-all-start.1 = ((bf16[128,32,224]{0,2,1:T(8,128)(2,1)}), bf16[128,32,224]{0,2,1:T(8,128)(2,1)}, u32[]{:S(2)}, u32[]{:S(2)}) async-start(bf16[128,32,224]{0,2,1:T(8,128)(2,1)} %bitcast.65), calls=%async_computation.1 | async-start | bytes 3670016 | tf_op jit(solution)/shard_map/all_to_all | solution.py:86
  322.8 24.2 %all-to-all-done.1 = bf16[128,32,224]{0,2,1:T(8,128)(2,1)} async-done(((bf16[128,32,224]{0,2,1:T(8,128)(2,1)}), bf16[128,32,224]{0,2,1:T(8,128)(2,1)}, u32[]{:S(2)}, u32[]{:S(2)}) %all-to-all-start.1) | async-done | bytes 1835040 | tf_op jit(solution)/shard_map/all_to_all | solution.py:86
  347.0 4.0 %copy.50 = bf16[32,128,224]{2,1,0:T(8,128)(2,1)} copy(bf16[32,128,224]{1,2,0:T(8,128)(2,1)} %bitcast.18) | data formatting | bytes 3670016 | tf_op jit(solution)/shard_map/all_to_all | solution.py:86
  351.0 8.5 %gather_fusion.1 = bf16[2048,224]{1,0:T(8,128)(2,1)S(1)} fusion(bf16[4096,224]{1,0:T(8,128)(2,1)} %bitcast.61, s32[2048]{0:T(1024)S(1)} %broadcast_clamp_fusion.1), kind=kCustom, calls=%fused_computation.1 | custom fusion | bytes 1843200 | tf_op jit(solution)/shard_map/gather | solution.py:87
  359.5 1.6 fusion.9
  (48 shorter events, 6.4 us)
Async XLA Ops:
  6.5 63.8 %copy-start = (bf16[4096,224]{0,1:T(8,128)(2,1)S(1)}, bf16[4096,224]{0,1:T(8,128)(2,1)}, u32[]{:S(2)}) copy-start(bf16[4096,224]{0,1:T(8,128)(2,1)} %param.16) | copy-start | bytes 5505028
  6.5 63.8 %all-gather.2.cloned.1.call-start = ((), (), s32[]{:S(2)}) async-start(), calls=%async_computation.2 | async-start | bytes 2162688 | tf_op jit(solution)/shard_map/all_gather | solution.py:59
  19.2 3.7 copy-start.5
  22.9 89.3 %all-reduce.3.cloned.1.call-start = ((), (), s32[]{:S(2)}) async-start(), calls=%async_computation.3 | async-start | bytes 458752 | tf_op jit(solution)/shard_map/psum | solution.py:63
  41.6 70.6 %copy-start.4 = (bf16[256,224]{0,1:T(8,128)(2,1)S(1)}, bf16[256,224]{0,1:T(8,128)(2,1)}, u32[]{:S(2)}) copy-start(bf16[256,224]{0,1:T(8,128)(2,1)} %param.17) | copy-start | bytes 344068
  41.6 136.6 %copy-start.7 = (f32[224]{0:T(256)S(1)}, f32[224]{0:T(256)}, u32[]{:S(2)}) copy-start(f32[224]{0:T(256)} %param.18) | copy-start | bytes 2692
  202.3 32.6 %copy-start.2 = (bf16[1,7168,256]{2,1,0:T(8,128)(2,1)S(1)}, bf16[1,7168,256]{2,1,0:T(8,128)(2,1)}, u32[]{:S(2)}) copy-start(bf16[1,7168,256]{2,1,0:T(8,128)(2,1)} %param.21) | copy-start | bytes 11010052
  233.7 1.3 copy-start.1
  315.2 6.9 %copy-start.6 = (f32[256,8]{0,1:T(8,128)S(1)}, f32[256,8]{0,1:T(8,128)}, u32[]{:S(2)}) copy-start(f32[256,8]{0,1:T(8,128)} %param.20) | copy-start | bytes 24580
  315.2 31.8 %all-to-all-start.1 = ((bf16[128,32,224]{0,2,1:T(8,128)(2,1)}), bf16[128,32,224]{0,2,1:T(8,128)(2,1)}, u32[]{:S(2)}, u32[]{:S(2)}) async-start(bf16[128,32,224]{0,2,1:T(8,128)(2,1)} %bitcast.65), calls=%async_computation.1 | async-start | bytes 3670016 | tf_op jit(solution)/shard_map/all_to_all | solution.py:86
  351.0 10.3 %copy-start.3 = (f32[256,224]{0,1:T(8,128)S(1)}, f32[256,224]{0,1:T(8,128)}, u32[]{:S(2)}) copy-start(f32[256,224]{0,1:T(8,128)} %all-reduce.3.cloned.1.call-done) | copy-start | bytes 688132
Sparse Core Ops, SparseCore 0:
  23.0 47.3 all-gather.1
  73.6 38.5 all-reduce.2
where the time goes:
time: 370 us; the launch traced here: 369 us
  blocking collectives  164 us (44%)
  waiting for transfers between devices  82.3 us (22%)
  local copies, waits for them, and re-layouts  58.4 us (16%)
  matrix products  26.6 us (7%)
  other arithmetic  16.7 us (5%)
  between operations  13.6 us (4%)
  starting transfers between devices  6.89 us (2%)
    psum x1, blocking collectives, per_device(): lax.psum(jnp.dot(hidden_units, down_weight[0], preferred_element_type=jnp...  67.9 us
    psum x1, blocking collectives, per_device(): squares = lax.psum(jnp.sum(stream * stream, axis=1), 'ep')  65 us
    all_to_all x1, blocking collectives, per_device(): lax.all_to_all(outgoing, 'ep', split_axis=1, concat_axis=1, tiled=True)  31.3 us
    psum x1, waiting for transfers between devices, per_device(): attention = lax.psum(partial_attn, 'head')  29.3 us
    all_gather x1, waiting for transfers between devices, per_device(): lax.all_gather(values, 'ep', axis=0, tiled=True)  28.8 us
    all_to_all x1, waiting for transfers between devices, per_device(): lax.all_to_all(summed, 'ep', split_axis=1, concat_axis=0, tiled=True)  24.2 us
    gather x2, local copies, waits for them, and re-layouts, per_device(): normed[slot_table]  21.4 us
    another operation x2, other arithmetic  9.27 us
  transfers between devices with their start and end apart: 3, of which 3 were waited for; matrix products, arithmetic and copies ran while one was open for 8% of the time, Pallas kernels for 0%

commit v1 on v0

v1 whole, which is shorter than its diff:
```python
import jax
import jax.numpy as jnp
from jax import lax
from jax.experimental import pallas as pl
from jax.experimental.pallas import tpu as pltpu
from jax.sharding import PartitionSpec as P

D = 7168
SCORE_SCALE = 192.0 ** (-0.5)
NORM_EPS = 1e-06

TOKENS = 256
EXPERTS = 32
SLOTS = 128
COLS = 224
ROWS = 240
GROUP = 4
TOPK = 8

BF16 = jnp.bfloat16
F32 = jnp.float32

NT = (((1,), (1,)), ((), ()))
NN = (((1,), (0,)), ((), ()))
TN = (((0,), (0,)), ((), ()))


def dot(a, b, dims):
    return lax.dot_general(a, b, dims, preferred_element_type=F32)


def slot_onehot(rank_row):
    slots = lax.broadcasted_iota(jnp.int32, (SLOTS, TOKENS), 0).astype(F32)
    return jnp.where(slots == rank_row, 1.0, 0.0).astype(BF16)


def route_kernel(me_ref, ids_ref, weight_ref, rank_ref, slot_weight_ref, token_weight):
    experts = lax.broadcasted_iota(jnp.int32, (EXPERTS, TOKENS), 0)
    member = jnp.zeros((EXPERTS, TOKENS), F32)
    weight = jnp.zeros((EXPERTS, TOKENS), F32)
    for k in range(TOPK):
        hit = experts == ids_ref[k : k + 1, :]
        member = jnp.where(hit, 1.0, member)
        weight = jnp.where(hit, weight_ref[k : k + 1, :], weight)
    before = lax.broadcasted_iota(jnp.int32, (TOKENS, TOKENS), 0)
    after = lax.broadcasted_iota(jnp.int32, (TOKENS, TOKENS), 1)
    earlier = jnp.where(before < after, 1.0, 0.0).astype(BF16)
    rank = dot(member.astype(BF16), earlier, NN)
    rank_ref[...] = jnp.where(member > 0.0, rank, -1.0)
    token_weight[...] = weight
    me = me_ref[0]
    slots = lax.broadcasted_iota(jnp.int32, (SLOTS, TOKENS), 0).astype(F32)
    mine = slots == rank_ref[pl.ds(me, 1), :]
    held = jnp.where(mine, token_weight[pl.ds(me, 1), :], 0.0)
    slot_weight_ref[...] = jnp.broadcast_to(
        jnp.sum(held, axis=1, keepdims=True), (SLOTS, 128)
    )


def route(me, ids_t, weight_t):
    vmem = pl.BlockSpec(memory_space=pltpu.VMEM)
    return pl.pallas_call(
        route_kernel,
        out_shape=(
            jax.ShapeDtypeStruct((EXPERTS, TOKENS), F32),
            jax.ShapeDtypeStruct((SLOTS, 128), F32),
        ),
        in_specs=[pl.BlockSpec(memory_space=pltpu.SMEM), vmem, vmem],
        out_specs=(vmem, vmem),
        scratch_shapes=[pltpu.VMEM((EXPERTS, TOKENS), F32)],
        name="route",
    )(me, ids_t, weight_t)


def project_kernel(me_ref, weight_ref, mine_ref, other_ref, out_ref):
    core = lax.rem(me_ref[0], 2)
    half = TOKENS // 2
    column = lax.broadcasted_iota(jnp.int32, (TOKENS, TOKENS), 0)
    token = lax.broadcasted_iota(jnp.int32, (TOKENS, TOKENS), 1)
    second = (column >= half).astype(jnp.int32)
    within = column - second * half
    parity = jnp.where(second == 1, 1 - core, core)
    owner = ((within >> 3) * 2 + parity) * 8 + (within & 7)
    order = jnp.where(owner == token, 1.0, 0.0).astype(BF16)
    weight = weight_ref[...]
    first = dot(weight, mine_ref[...], NT).astype(BF16)
    last = dot(weight, other_ref[...], NT).astype(BF16)
    placed = dot(first, order[:half], NN) + dot(last, order[half:], NN)
    out_ref[...] = placed.astype(BF16)


def project(me, weight_t, mine, other):
    vmem = pl.BlockSpec(memory_space=pltpu.VMEM)
    return pl.pallas_call(
        project_kernel,
        out_shape=jax.ShapeDtypeStruct((COLS, TOKENS), BF16),
        in_specs=[pl.BlockSpec(memory_space=pltpu.SMEM), vmem, vmem, vmem],
        out_specs=vmem,
        compiler_params=pltpu.CompilerParams(vmem_limit_bytes=32 * 2**20),
        name="project",
    )(me, weight_t, mine, other)


def dispatch_kernel(p0, p1, p2, p3, residual_ref, gain_ref, rank_ref, stream_ref, out_ref):
    attention = (p0[...].astype(F32) + p2[...].astype(F32)) + (
        p1[...].astype(F32) + p3[...].astype(F32)
    )
    stream = residual_ref[...].astype(F32) + attention
    stream_ref[...] = stream
    squares = jnp.sum(stream * stream, axis=0, keepdims=True)
    high = squares.astype(BF16).astype(F32)
    low = squares - high
    tail = lax.broadcasted_iota(jnp.int32, (ROWS - COLS, TOKENS), 0)
    tail = jnp.where(tail == 0, high, jnp.where(tail == 1, low, 0.0))
    scaled = (stream * gain_ref[...]).astype(BF16)
    rows = jnp.concatenate([scaled, tail.astype(BF16)], axis=0)
    for e in range(EXPERTS):
        chosen = slot_onehot(rank_ref[e : e + 1, :])
        out_ref[e] = dot(rows, chosen, NT).astype(BF16)


def dispatch(parts, residual_t, gain, rank):
    vmem = pl.BlockSpec(memory_space=pltpu.VMEM)
    return pl.pallas_call(
        dispatch_kernel,
        out_shape=(
            jax.ShapeDtypeStruct((COLS, TOKENS), F32),
            jax.ShapeDtypeStruct((EXPERTS, ROWS, SLOTS), BF16),
        ),
        in_specs=[vmem] * 7,
        out_specs=(vmem, vmem),
        compiler_params=pltpu.CompilerParams(vmem_limit_bytes=32 * 2**20),
        name="dispatch",
    )(*parts, residual_t, gain, rank)


def expert_kernel(
    tail_ref, slot_weight_ref, rows_ref, gate_ref, up_ref, down_ref, out_ref, gate_sum, up_sum, hidden
):
    step = pl.program_id(0)
    steps = EXPERTS // GROUP

    @pl.when(step == 0)
    def _():
        gate_sum[...] = jnp.zeros_like(gate_sum)
        up_sum[...] = jnp.zeros_like(up_sum)

    @pl.when(step < steps)
    def _():
        gate = gate_sum[...]
        up = up_sum[...]
        for j in range(GROUP):
            rows = rows_ref[j, :COLS, :]
            gate = gate + dot(rows, gate_ref[j * COLS : (j + 1) * COLS, :], TN)
            up = up + dot(rows, up_ref[j * COLS : (j + 1) * COLS, :], TN)
        gate_sum[...] = gate
        up_sum[...] = up

    @pl.when(step == steps - 1)
    def _():
        parts = jnp.sum(tail_ref[...].astype(F32), axis=0)
        squares = jnp.sum(parts, axis=0, keepdims=True)
        factor = lax.rsqrt(squares / D + NORM_EPS)
        row = lax.broadcasted_iota(jnp.int32, (SLOTS, SLOTS), 0)
        column = lax.broadcasted_iota(jnp.int32, (SLOTS, SLOTS), 1)
        factor = jnp.sum(jnp.where(row == column, factor, 0.0), axis=1, keepdims=True)
        gate = gate_sum[...] * factor
        up = up_sum[...] * factor
        value = gate / (1.0 + jnp.exp(-gate)) * up
        hidden[...] = (value * slot_weight_ref[:, :1]).astype(BF16)

    @pl.when(step >= steps)
    def _():
        result = dot(hidden[...], down_ref[...], NN)
        out_ref[...] = result.T.astype(BF16).reshape(GROUP, COLS, SLOTS)


def expert(tail, slot_weight, rows, gate_weight, up_weight, down_weight):
    steps = EXPERTS // GROUP
    width = gate_weight.shape[1]
    whole = lambda *shape: pl.BlockSpec(shape, lambda i: (0,) * len(shape))
    first = lambda i: jnp.minimum(i, steps - 1)
    second = lambda i: jnp.maximum(i - steps, 0)
    return pl.pallas_call(
        expert_kernel,
        grid=(2 * steps,),
        out_shape=jax.ShapeDtypeStruct((EXPERTS, COLS, SLOTS), BF16),
        in_specs=[
            whole(EXPERTS, ROWS - COLS, SLOTS),
            whole(SLOTS, 128),
            pl.BlockSpec((GROUP, ROWS, SLOTS), lambda i: (first(i), 0, 0)),
            pl.BlockSpec((GROUP * COLS, width), lambda i: (first(i), 0)),
            pl.BlockSpec((GROUP * COLS, width), lambda i: (first(i), 0)),
            pl.BlockSpec((width, GROUP * COLS), lambda i: (0, second(i))),
        ],
        out_specs=pl.BlockSpec((GROUP, COLS, SLOTS), lambda i: (second(i), 0, 0)),
        scratch_shapes=[
            pltpu.VMEM((SLOTS, width), F32),
            pltpu.VMEM((SLOTS, width), F32),
            pltpu.VMEM((SLOTS, width), BF16),
        ],
        compiler_params=pltpu.CompilerParams(vmem_limit_bytes=32 * 2**20),
        name="expert",
    )(tail, slot_weight, rows, gate_weight, up_weight, down_weight)


def combine_kernel(returned_ref, rank_ref, out_ref):
    total = jnp.zeros((COLS, TOKENS), F32)
    for e in range(EXPERTS):
        total = total + dot(returned_ref[e], slot_onehot(rank_ref[e : e + 1, :]), NN)
    out_ref[...] = total.astype(BF16)


def combine(returned, rank):
    vmem = pl.BlockSpec(memory_space=pltpu.VMEM)
    return pl.pallas_call(
        combine_kernel,
        out_shape=jax.ShapeDtypeStruct((COLS, TOKENS), BF16),
        in_specs=[vmem, vmem],
        out_specs=vmem,
        compiler_params=pltpu.CompilerParams(vmem_limit_bytes=32 * 2**20),
        name="combine",
    )(returned, rank)


def around_z(part):
    size = lax.axis_size("head")
    return [part] + [
        lax.ppermute(part, "head", [(z, (z + step) % size) for z in range(size)])
        for step in range(1, size)
    ]


def per_device(
    queries,
    latent_cache,
    lengths,
    value_up,
    output_weight,
    residual,
    norm_gain,
    expert_ids,
    expert_weight,
    gate_weight,
    up_weight,
    down_weight,
):
    local_seqs = queries.shape[0]
    me = lax.axis_index("ep").astype(jnp.int32).reshape(1)
    rank, slot_weight = route(me, expert_ids.T, expert_weight.T)

    positions = jnp.arange(latent_cache.shape[1], dtype=jnp.int32)
    scores = (
        jnp.einsum("shd,scd->shc", queries, latent_cache, preferred_element_type=jnp.float32)
        * SCORE_SCALE
    )
    allowed = (positions[None, :] < lengths[:, None])[:, None, :]
    scores = jnp.where(allowed, scores, jnp.float32(-1e30))
    row_peaks = jnp.max(scores, axis=2, keepdims=True)
    exponents = jnp.exp(scores - row_peaks)
    attn_weights = (exponents / jnp.sum(exponents, axis=2, keepdims=True)).astype(jnp.bfloat16)
    latent_width = value_up.shape[1]
    contexts = jnp.einsum(
        "shc,scl->shl",
        attn_weights,
        latent_cache[:, :, :latent_width],
        preferred_element_type=jnp.float32,
    ).astype(jnp.bfloat16)
    values = jnp.einsum("shl,hlv->shv", contexts, value_up, preferred_element_type=jnp.float32)
    values = values.astype(jnp.bfloat16).reshape(local_seqs, -1)

    chips = EXPERTS // 2
    same_core = [[2 * chip + core for chip in range(chips)] for core in range(2)]
    copies = jnp.broadcast_to(values[None], (chips,) + values.shape)
    mine = lax.all_to_all(
        copies, "ep", split_axis=0, concat_axis=0, tiled=True, axis_index_groups=same_core
    ).reshape(chips * local_seqs, -1)
    other = lax.ppermute(mine, "ep", [(i, i ^ 1) for i in range(EXPERTS)])
    partial = project(me, output_weight.T, mine, other)

    stream, outgoing = dispatch(around_z(partial), residual.T, norm_gain[:, None], rank)
    arrived = lax.all_to_all(outgoing, "ep", split_axis=0, concat_axis=0, tiled=True)
    results = expert(
        arrived[:, COLS:, :], slot_weight, arrived, gate_weight[0], up_weight[0], down_weight[0]
    )
    returned = lax.all_to_all(results, "ep", split_axis=0, concat_axis=0, tiled=True)
    c0, c1, c2, c3 = around_z(combine(returned, rank))
    combined = (c0.astype(F32) + c2.astype(F32)) + (c1.astype(F32) + c3.astype(F32))
    return (stream + combined).astype(BF16).T


def solution(mesh):
    placed = (
        P("ep", "head", None),
        P("ep", None, None),
        P("ep"),
        P("head", None, None),
        P("head", "ep"),
        P(None, "ep"),
        P("ep"),
        P(),
        P(),
        P("ep", None, "head"),
        P("ep", None, "head"),
        P("ep", "head", None),
    )
    return jax.shard_map(
        per_device, mesh=mesh, in_specs=placed, out_specs=P(None, "ep"), check_vma=False
    )
```

time: 370 us -> 141 us (0.38)
  blocking collectives: 164 us -> 83.3 us
  waiting for transfers between devices: 82.3 us -> 13.2 us
  local copies, waits for them, and re-layouts: 58.4 us -> 5.31 us
  other arithmetic: 16.7 us -> 1.81 us
  between operations: 13.6 us -> 0.12 us
  Pallas kernels: 0 us -> 12.5 us
  matrix products: 26.6 us -> 14.4 us
    psum x2 -> x0, blocking collectives: 133 us -> none  [the longest x1 67.9 us: per_device(): lax.psum(jnp.dot(hidden_units, down_weight[0], preferred_element_type=jnp...]
    all_to_all x1 -> x3, blocking collectives: 31.3 us -> 83.3 us  [the longest x1 30.8 us: per_device(): lax.all_to_all(outgoing, 'ep', split_axis=0, concat_axis=0, tiled=True)]
    gather x3 -> x0, local copies, waits for them, and re-layouts: 29.9 us -> none  [the longest x2 21.4 us: per_device(): normed[slot_table]]
    psum x1 -> x0, waiting for transfers between devices: 29.3 us -> none  [per_device(): attention = lax.psum(partial_attn, 'head')]
    all_gather x1 -> x0, waiting for transfers between devices: 28.8 us -> none  [per_device(): lax.all_gather(values, 'ep', axis=0, tiled=True)]
    all_to_all x1 -> x0, waiting for transfers between devices: 24.2 us -> none  [per_device(): lax.all_to_all(summed, 'ep', split_axis=1, concat_axis=0, tiled=True)]
    scatter x2 -> x0, local copies, waits for them, and re-layouts: 17.2 us -> none  [the longest x1 9.13 us: routing_slots(): jnp.zeros((experts * capacity,), jnp.bool_).at[destination].set(True)]
    ppermute x0 -> x7, waiting for transfers between devices: none -> 13.2 us  [the longest x6 10.8 us: around_z(): lax.ppermute(part, 'head', [(z, (z + step) % size) for z in range(size)])]
  transfers between devices with their start and end apart: 3 -> 7, of which waited for: 3 -> 7; matrix products, arithmetic and copies ran while one was open for 8% -> 0% of each run, Pallas kernels for 0% -> 1%
where the time goes in v1:
time: 141 us; the launch traced here: 139 us
  blocking collectives  83.3 us (59%)
  matrix products  14.4 us (10%)
  waiting for transfers between devices  13.2 us (9%)
  Pallas kernels  12.5 us (9%)
  starting transfers between devices  8.47 us (6%)
  local copies, waits for them, and re-layouts  5.31 us (4%)
  other arithmetic  1.81 us (1%)
    all_to_all x1, blocking collectives, per_device(): lax.all_to_all(outgoing, 'ep', split_axis=0, concat_axis=0, tiled=True)  30.8 us
    all_to_all x1, blocking collectives, per_device(): lax.all_to_all(results, 'ep', split_axis=0, concat_axis=0, tiled=True)  29 us
    all_to_all x1, blocking collectives, per_device(): lax.all_to_all(copies, 'ep', split_axis=0, concat_axis=0, tiled=True, axi...  23.5 us
    ppermute x6, waiting for transfers between devices, around_z(): lax.ppermute(part, 'head', [(z, (z + step) % size) for z in range(size)])  10.8 us
    ppermute x6, starting transfers between devices, around_z(): lax.ppermute(part, 'head', [(z, (z + step) % size) for z in range(size)])  6.48 us
    pallas_call x1, Pallas kernels, expert(): pl.pallas_call(expert_kernel, grid=(2 * steps,), out_shape=jax.ShapeDtype...  6.06 us
    dot_general x1, matrix products, per_device(): jnp.einsum('shc,scl->shl', attn_weights, latent_cache[:, :, :latent_width...  6.01 us
    dot_general x1, matrix products, per_device(): jnp.einsum('shd,scd->shc', queries, latent_cache, preferred_element_type=...  5.38 us
  transfers between devices with their start and end apart: 7, of which 7 were waited for; matrix products, arithmetic and copies ran while one was open for 0% of the time, Pallas kernels for 1%

profile of v1, /device:TPU:1, one launch (start us, length us, event | category | flops | bytes accessed | tf_op | source)
XLA Modules:
  0.0 139.2 jit_solution(5086900863967862295)
XLA Ops:
  0.0 0.8 iota_compare_fusion
  1.0 5.4 %fusion.5 = f32[8,32,1024]{2,1,0:T(8,128)S(1)} fusion(bf16[8,32,576]{2,1,0:T(8,128)(2,1)S(1)} %copy-done, bf16[8,1024,576]{1,2,0:T(8,128)(2,1)} %param.13, pred[8,1024]{1,0:T(8,128)(4,1)S(1)} %iota_compare_fusion), kind=kOutput, calls=%fused_computation.6 | convolution fusion | flops 302514176 | bytes 10788864 | tf_op jit(solution)/shard_map/shd,scd->shc/dot_general | solution.py:254
  6.7 6.0 %fusion.1 = bf16[8,32,512]{2,1,0:T(8,128)(2,1)S(1)} fusion(bf16[8,1024,576]{1,2,0:T(8,128)(2,1)} %param.13, f32[8,32]{1,0:T(8,128)S(1)} %fusion.10, f32[8,32,1024]{2,1,0:T(8,128)S(1)} %fusion.5), kind=kOutput, calls=%fused_computation.1 | convolution fusion | flops 269223168 | bytes 10752000 | tf_op jit(solution)/shard_map/shc,scl->shl/dot_general | solution.py:263
  12.7 3.0 %fusion.6 = bf16[8,4096]{1,0:T(8,128)(2,1)S(1)} fusion(bf16[32,512,128]{2,1,0:T(8,128)(2,1)} %param.15, bf16[8,32,512]{2,1,0:T(8,128)(2,1)S(1)} %fusion.1), kind=kOutput, calls=%fused_computation.8 | convolution fusion | flops 33587200 | bytes 4521984 | tf_op jit(solution)/shard_map/shl,hlv->shv/dot_general | solution.py:269
  15.9 23.5 %all_to_all.15 = bf16[16,8,4096]{2,1,0:T(8,128)(2,1)S(1)} all-to-all(bf16[16,8,4096]{2,1,0:T(8,128)(2,1)S(1)} %broadcast_in_dim.30), channel_id=1, replica_groups={{0,8,16,24,32,40,48,56,64,72,80,88,96,104,112,120},{4,12,20,28,36,44,52..., dimensions={0} | all-to-all | bytes 2097152 | tf_op jit(solution)/shard_map/all_to_all | solution.py:275
  39.4 2.0 %collective-permute-start = (bf16[128,4096]{1,0:T(8,128)(2,1)S(1)}, bf16[128,4096]{1,0:T(8,128)(2,1)}, u32[]{:S(2)}, u32[]{:S(2)}) collective-permute-start(bf16[128,4096]{1,0:T(8,128)(2,1)S(1)} %bitcast.21), channel_id=1, source_target_pairs={{0,4},{4,0},{8,12},{12,8},{16,20},{20,16},{24,28},{28,24},{32,36},... | collective-permute-start | bytes 3145736 | tf_op jit(solution)/shard_map/ppermute | solution.py:278
  41.4 2.4 %collective-permute-done.other_ref = bf16[128,4096]{1,0:T(8,128)(2,1)} collective-permute-done((bf16[128,4096]{1,0:T(8,128)(2,1)S(1)}, bf16[128,4096]{1,0:T(8,128)(2,1)}, u32[]{:S(2)}, u32[]{:S(2)}) %collective-permute-start) | collective-permute-done | bytes 1048608 | tf_op jit(solution)/shard_map/ppermute | solution.py:278
  43.8 2.6 %project.1.p0 = bf16[224,256]{1,0:T(8,128)(2,1)S(1)} custom-call(s32[1]{0:T(128)} %bitcast.me_ref, bf16[224,4096]{1,0:T(8,128)(2,1)S(1)} %bitcast.26, bf16[128,4096]{1,0:T(8,128)(2,1)S(1)} %bitcast.22, bf16[128,4096]{1,0:T(8,128)(2,1)} %collective-permute-done.other_ref), custom_call_target="tpu_custom_call" | custom-call | tf_op jit(solution)/shard_map/project/pallas_call | solution.py:94
  46.4 3.8 %collective-permute-start.3 = (bf16[224,256]{1,0:T(8,128)(2,1)S(1)}, bf16[224,256]{1,0:T(8,128)(2,1)S(1)}, u32[]{:S(2)}, u32[]{:S(2)}) collective-permute-start(bf16[224,256]{1,0:T(8,128)(2,1)S(1)} %project.1.p0), channel_id=1, source_target_pairs={{0,3},{1,0},{2,1},{3,2},{4,7},{5,4},{6,5},{7,6},{8,11},{9,8},{10,9... | collective-permute-start | bytes 344072 | tf_op jit(solution)/shard_map/ppermute | solution.py:229
  51.1 1.6 %route.1 = (f32[32,256]{1,0:T(8,128)}, f32[128,128]{1,0:T(8,128)}) custom-call(s32[1]{0:T(128)} %bitcast.me_ref, s32[8,256]{1,0:T(8,128)} %bitcast.28, f32[8,256]{1,0:T(8,128)} %bitcast.29), custom_call_target="tpu_custom_call" | custom-call | tf_op jit(solution)/shard_map/route/pallas_call | solution.py:62
  52.7 2.5 %collective-permute-done.3.p3 = bf16[224,256]{1,0:T(8,128)(2,1)S(1)} collective-permute-done((bf16[224,256]{1,0:T(8,128)(2,1)S(1)}, bf16[224,256]{1,0:T(8,128)(2,1)S(1)}, u32[]{:S(2)}, u32[]{:S(2)}) %collective-permute-start.3) | collective-permute-done | bytes 114720 | tf_op jit(solution)/shard_map/ppermute | solution.py:229
  55.9 2.8 %collective-permute-done.1.p1 = bf16[224,256]{1,0:T(8,128)(2,1)S(1)} collective-permute-done((bf16[224,256]{1,0:T(8,128)(2,1)S(1)}, bf16[224,256]{1,0:T(8,128)(2,1)S(1)}, u32[]{:S(2)}, u32[]{:S(2)}) %collective-permute-start.1) | collective-permute-done | bytes 114720 | tf_op jit(solution)/shard_map/ppermute | solution.py:229
  58.7 0.8 copy-done.5
  59.4 1.2 dispatch.1
  60.7 30.8 %all_to_all.16.rows_ref = bf16[32,240,128]{2,1,0:T(8,128)(2,1)S(1)} all-to-all(bf16[32,240,128]{2,1,0:T(8,128)(2,1)S(1)} %get-tuple-element.11), channel_id=1, replica_groups=mesh['ep'=32,'head'=4] {'ep'}, dimensions={0} | all-to-all | bytes 3932160 | tf_op jit(solution)/shard_map/all_to_all | solution.py:282
  91.5 2.0 %copy-done.2 = bf16[1,7168,256]{2,1,0:T(8,128)(2,1)S(1)} copy-done((bf16[1,7168,256]{2,1,0:T(8,128)(2,1)S(1)}, bf16[1,7168,256]{2,1,0:T(8,128)(2,1)}, u32[]{:S(2)}) %copy-start.2) | copy-done | bytes 3670040
  93.5 2.0 %copy-done.3 = bf16[1,256,7168]{2,1,0:T(8,128)(2,1)S(1)} copy-done((bf16[1,256,7168]{2,1,0:T(8,128)(2,1)S(1)}, bf16[1,256,7168]{2,1,0:T(8,128)(2,1)}, u32[]{:S(2)}) %copy-start.3) | copy-done | bytes 3670040
  95.6 6.1 %expert.1 = bf16[32,224,128]{2,1,0:T(8,128)(2,1)S(1)} custom-call(bf16[32,16,128]{2,1,0:T(8,128)(2,1)S(1)} %slice.8.tail_ref, f32[128,128]{1,0:T(8,128)S(1)} %copy-done.8, bf16[32,240,128]{2,1,0:T(8,128)(2,1)S(1)} %all_to_all.16.rows_ref, bf16[7168,256]{1,0:T(8,128)(2,1)S(1)} %bitcast.23, bf16[7168,256]{1,0:T(8,128)(2,1)S(1)} %bitcast.24, ...), custom_call_target="tpu_custom_call" | custom-call | tf_op jit(solution)/shard_map/expert/pallas_call | solution.py:184
  101.6 29.0 %all_to_all.17.returned_ref = bf16[32,224,128]{2,1,0:T(8,128)(2,1)S(1)} all-to-all(bf16[32,224,128]{2,1,0:T(8,128)(2,1)S(1)} %expert.1), channel_id=1, replica_groups=mesh['ep'=32,'head'=4] {'ep'}, dimensions={0} | all-to-all | bytes 3670016 | tf_op jit(solution)/shard_map/all_to_all | solution.py:286
  130.6 1.1 combine.1
  132.4 0.8 collective-permute-start.5
  133.7 2.2 %collective-permute-done.6 = bf16[224,256]{1,0:T(8,128)(2,1)S(1)} collective-permute-done((bf16[224,256]{1,0:T(8,128)(2,1)S(1)}, bf16[224,256]{1,0:T(8,128)(2,1)S(1)}, u32[]{:S(2)}, u32[]{:S(2)}) %collective-permute-start.6) | collective-permute-done | bytes 114720 | tf_op jit(solution)/shard_map/ppermute | solution.py:229
  135.9 1.4 collective-permute-done.5
  137.3 1.2 collective-permute-done.4
  (27 shorter events, 4.0 us)
Async XLA Ops:
  0.0 1.0 copy-start
  12.7 31.1 %copy-start.4 = (bf16[4096,224]{0,1:T(8,128)(2,1)S(1)}, bf16[4096,224]{0,1:T(8,128)(2,1)}, u32[]{:S(2)}) copy-start(bf16[4096,224]{0,1:T(8,128)(2,1)} %param.16) | copy-start | bytes 5505028
  15.8 35.1 %copy-start.9 = (f32[224]{0:T(256)S(1)}, f32[224]{0:T(256)}, u32[]{:S(2)}) copy-start(f32[224]{0:T(256)} %param.18) | copy-start | bytes 2692
  15.8 42.9 %copy-start.7 = (bf16[256,224]{0,1:T(8,128)(2,1)S(1)}, bf16[256,224]{0,1:T(8,128)(2,1)}, u32[]{:S(2)}) copy-start(bf16[256,224]{0,1:T(8,128)(2,1)} %param.17) | copy-start | bytes 344068
  39.4 4.4 %collective-permute-start = (bf16[128,4096]{1,0:T(8,128)(2,1)S(1)}, bf16[128,4096]{1,0:T(8,128)(2,1)}, u32[]{:S(2)}, u32[]{:S(2)}) collective-permute-start(bf16[128,4096]{1,0:T(8,128)(2,1)S(1)} %bitcast.21), channel_id=1, source_target_pairs={{0,4},{4,0},{8,12},{12,8},{16,20},{20,16},{24,28},{28,24},{32,36},... | collective-permute-start | bytes 3145736 | tf_op jit(solution)/shard_map/ppermute | solution.py:278
  46.4 8.8 %collective-permute-start.3 = (bf16[224,256]{1,0:T(8,128)(2,1)S(1)}, bf16[224,256]{1,0:T(8,128)(2,1)S(1)}, u32[]{:S(2)}, u32[]{:S(2)}) collective-permute-start(bf16[224,256]{1,0:T(8,128)(2,1)S(1)} %project.1.p0), channel_id=1, source_target_pairs={{0,3},{1,0},{2,1},{3,2},{4,7},{5,4},{6,5},{7,6},{8,11},{9,8},{10,9... | collective-permute-start | bytes 344072 | tf_op jit(solution)/shard_map/ppermute | solution.py:229
  50.2 5.6 %collective-permute-start.2 = (bf16[224,256]{1,0:T(8,128)(2,1)S(1)}, bf16[224,256]{1,0:T(8,128)(2,1)S(1)}, u32[]{:S(2)}, u32[]{:S(2)}) collective-permute-start(bf16[224,256]{1,0:T(8,128)(2,1)S(1)} %project.1.p0), channel_id=1, source_target_pairs={{0,2},{1,3},{2,0},{3,1},{4,6},{5,7},{6,4},{7,5},{8,10},{9,11},{10,... | collective-permute-start | bytes 344072 | tf_op jit(solution)/shard_map/ppermute | solution.py:229
  50.2 8.4 %collective-permute-start.1 = (bf16[224,256]{1,0:T(8,128)(2,1)S(1)}, bf16[224,256]{1,0:T(8,128)(2,1)S(1)}, u32[]{:S(2)}, u32[]{:S(2)}) collective-permute-start(bf16[224,256]{1,0:T(8,128)(2,1)S(1)} %project.1.p0), channel_id=1, source_target_pairs={{0,1},{1,2},{2,3},{3,0},{4,5},{5,6},{6,7},{7,4},{8,9},{9,10},{10,1... | collective-permute-start | bytes 344072 | tf_op jit(solution)/shard_map/ppermute | solution.py:229
  52.7 38.8 %copy-start.1 = (bf16[1,7168,256]{2,1,0:T(8,128)(2,1)S(1)}, bf16[1,7168,256]{2,1,0:T(8,128)(2,1)}, u32[]{:S(2)}) copy-start(bf16[1,7168,256]{2,1,0:T(8,128)(2,1)} %param.21) | copy-start | bytes 11010052
  58.7 0.8 copy-start.5
  59.4 32.1 %copy-start.8 = (f32[128,128]{1,0:T(8,128)S(1)}, f32[128,128]{1,0:T(8,128)}, u32[]{:S(2)}) copy-start(f32[128,128]{1,0:T(8,128)} %get-tuple-element.12.slot_weight_ref) | copy-start | bytes 196612
  91.5 2.0 %copy-start.2 = (bf16[1,7168,256]{2,1,0:T(8,128)(2,1)S(1)}, bf16[1,7168,256]{2,1,0:T(8,128)(2,1)}, u32[]{:S(2)}) copy-start(bf16[1,7168,256]{2,1,0:T(8,128)(2,1)} %param.22) | copy-start | bytes 11010052
  93.5 2.0 %copy-start.3 = (bf16[1,256,7168]{2,1,0:T(8,128)(2,1)S(1)}, bf16[1,256,7168]{2,1,0:T(8,128)(2,1)}, u32[]{:S(2)}) copy-start(bf16[1,256,7168]{2,1,0:T(8,128)(2,1)} %param.23) | copy-start | bytes 11010052
  95.6 35.1 %copy-start.6 = (f32[32,256]{1,0:T(8,128)S(1)}, f32[32,256]{1,0:T(8,128)}, u32[]{:S(2)}) copy-start(f32[32,256]{1,0:T(8,128)} %get-tuple-element.9.rank_ref) | copy-start | bytes 98308
  131.7 4.2 %collective-permute-start.6 = (bf16[224,256]{1,0:T(8,128)(2,1)S(1)}, bf16[224,256]{1,0:T(8,128)(2,1)S(1)}, u32[]{:S(2)}, u32[]{:S(2)}) collective-permute-start(bf16[224,256]{1,0:T(8,128)(2,1)S(1)} %combine.1), channel_id=1, source_target_pairs={{0,3},{1,0},{2,1},{3,2},{4,7},{5,4},{6,5},{7,6},{8,11},{9,8},{10,9... | collective-permute-start | bytes 344072 | tf_op jit(solution)/shard_map/ppermute | solution.py:229
  132.4 4.9 %collective-permute-start.5 = (bf16[224,256]{1,0:T(8,128)(2,1)S(1)}, bf16[224,256]{1,0:T(8,128)(2,1)S(1)}, u32[]{:S(2)}, u32[]{:S(2)}) collective-permute-start(bf16[224,256]{1,0:T(8,128)(2,1)S(1)} %combine.1), channel_id=1, source_target_pairs={{0,1},{1,2},{2,3},{3,0},{4,5},{5,6},{6,7},{7,4},{8,9},{9,10},{10,1... | collective-permute-start | bytes 344072 | tf_op jit(solution)/shard_map/ppermute | solution.py:229
  133.3 5.3 %collective-permute-start.4 = (bf16[224,256]{1,0:T(8,128)(2,1)S(1)}, bf16[224,256]{1,0:T(8,128)(2,1)S(1)}, u32[]{:S(2)}, u32[]{:S(2)}) collective-permute-start(bf16[224,256]{1,0:T(8,128)(2,1)S(1)} %combine.1), channel_id=1, source_target_pairs={{0,2},{1,3},{2,0},{3,1},{4,6},{5,7},{6,4},{7,5},{8,10},{9,11},{10,... | collective-permute-start | bytes 344072 | tf_op jit(solution)/shard_map/ppermute | solution.py:229

commit v2 on v1

v2 whole, which is shorter than its diff:
```python
import jax
import jax.numpy as jnp
from jax import lax
from jax.experimental import pallas as pl
from jax.experimental.pallas import tpu as pltpu
from jax.sharding import PartitionSpec as P

D = 7168
SCORE_SCALE = 192.0 ** (-0.5)
NORM_EPS = 1e-06

TOKENS = 256
EXPERTS = 32
SLOTS = 128
COLS = 224
ROWS = 240
GROUP = 4
TOPK = 8
SEQS = 2

BF16 = jnp.bfloat16
F32 = jnp.float32

NT = (((1,), (1,)), ((), ()))
NN = (((1,), (0,)), ((), ()))
TN = (((0,), (0,)), ((), ()))


def dot(a, b, dims):
    return lax.dot_general(a, b, dims, preferred_element_type=F32)


def attend_kernel(lengths_ref, queries_ref, cache_ref, up_hbm, out_ref, contexts, up_ref, up_sem):
    step = pl.program_id(0)
    heads, latent, width = up_ref.shape
    up_copy = pltpu.make_async_copy(up_hbm, up_ref, up_sem)

    @pl.when(step == 0)
    def _():
        up_copy.start()

    for b in range(SEQS):
        seq = step * SEQS + b
        scores = dot(queries_ref[b], cache_ref[b], NN) * SCORE_SCALE
        positions = lax.broadcasted_iota(jnp.int32, scores.shape, 1)
        scores = jnp.where(positions < lengths_ref[seq], scores, -1e30)
        exponents = jnp.exp(scores - jnp.max(scores, axis=1, keepdims=True))
        probs = (exponents / jnp.sum(exponents, axis=1, keepdims=True)).astype(BF16)
        contexts[seq] = dot(probs, cache_ref[b, :latent, :], NT)

    @pl.when(step == pl.num_programs(0) - 1)
    def _():
        up_copy.wait()
        for h in range(heads):
            rows = contexts[:, h, :].astype(BF16)
            out_ref[:, h * width : (h + 1) * width] = dot(rows, up_ref[h], NN).astype(BF16)


def attend(lengths, queries, cache_t, value_up):
    seqs, heads, kdim = queries.shape
    context = cache_t.shape[2]
    _, latent, width = value_up.shape
    return pl.pallas_call(
        attend_kernel,
        grid=(seqs // SEQS,),
        out_shape=jax.ShapeDtypeStruct((seqs, heads * width), BF16),
        in_specs=[
            pl.BlockSpec(memory_space=pltpu.SMEM),
            pl.BlockSpec((SEQS, heads, kdim), lambda i: (i, 0, 0)),
            pl.BlockSpec((SEQS, kdim, context), lambda i: (i, 0, 0)),
            pl.BlockSpec(memory_space=pl.ANY),
        ],
        out_specs=pl.BlockSpec((seqs, heads * width), lambda i: (0, 0)),
        scratch_shapes=[
            pltpu.VMEM((seqs, heads, latent), F32),
            pltpu.VMEM(value_up.shape, BF16),
            pltpu.SemaphoreType.DMA,
        ],
        compiler_params=pltpu.CompilerParams(vmem_limit_bytes=61 * 2**20),
        name="attend",
    )(lengths, queries, cache_t, value_up)


def slot_onehot(rank_row):
    slots = lax.broadcasted_iota(jnp.int32, (SLOTS, TOKENS), 0).astype(F32)
    return jnp.where(slots == rank_row, 1.0, 0.0).astype(BF16)


def route_kernel(me_ref, ids_ref, weight_ref, rank_ref, slot_weight_ref, token_weight):
    experts = lax.broadcasted_iota(jnp.int32, (EXPERTS, TOKENS), 0)
    member = jnp.zeros((EXPERTS, TOKENS), F32)
    weight = jnp.zeros((EXPERTS, TOKENS), F32)
    for k in range(TOPK):
        hit = experts == ids_ref[k : k + 1, :]
        member = jnp.where(hit, 1.0, member)
        weight = jnp.where(hit, weight_ref[k : k + 1, :], weight)
    before = lax.broadcasted_iota(jnp.int32, (TOKENS, TOKENS), 0)
    after = lax.broadcasted_iota(jnp.int32, (TOKENS, TOKENS), 1)
    earlier = jnp.where(before < after, 1.0, 0.0).astype(BF16)
    rank = dot(member.astype(BF16), earlier, NN)
    rank_ref[...] = jnp.where(member > 0.0, rank, -1.0)
    token_weight[...] = weight
    me = me_ref[0]
    slots = lax.broadcasted_iota(jnp.int32, (SLOTS, TOKENS), 0).astype(F32)
    mine = slots == rank_ref[pl.ds(me, 1), :]
    held = jnp.where(mine, token_weight[pl.ds(me, 1), :], 0.0)
    slot_weight_ref[...] = jnp.broadcast_to(
        jnp.sum(held, axis=1, keepdims=True), (SLOTS, 128)
    )


def route(me, ids_t, weight_t):
    vmem = pl.BlockSpec(memory_space=pltpu.VMEM)
    return pl.pallas_call(
        route_kernel,
        out_shape=(
            jax.ShapeDtypeStruct((EXPERTS, TOKENS), F32),
            jax.ShapeDtypeStruct((SLOTS, 128), F32),
        ),
        in_specs=[pl.BlockSpec(memory_space=pltpu.SMEM), vmem, vmem],
        out_specs=(vmem, vmem),
        scratch_shapes=[pltpu.VMEM((EXPERTS, TOKENS), F32)],
        name="route",
    )(me, ids_t, weight_t)


def half_kernel(weight_ref, values_ref, out_ref):
    out_ref[...] = dot(weight_ref[...], values_ref[...], NT).astype(BF16)


def project_half(weight_t, values):
    vmem = pl.BlockSpec(memory_space=pltpu.VMEM)
    return pl.pallas_call(
        half_kernel,
        out_shape=jax.ShapeDtypeStruct((COLS, values.shape[0]), BF16),
        in_specs=[vmem, vmem],
        out_specs=vmem,
        compiler_params=pltpu.CompilerParams(vmem_limit_bytes=16 * 2**20),
        name="project_half",
    )(weight_t, values)


def project_kernel(me_ref, weight_ref, first_ref, other_ref, out_ref):
    core = lax.rem(me_ref[0], 2)
    half = TOKENS // 2
    column = lax.broadcasted_iota(jnp.int32, (TOKENS, TOKENS), 0)
    token = lax.broadcasted_iota(jnp.int32, (TOKENS, TOKENS), 1)
    second = (column >= half).astype(jnp.int32)
    within = column - second * half
    parity = jnp.where(second == 1, 1 - core, core)
    owner = ((within >> 3) * 2 + parity) * 8 + (within & 7)
    order = jnp.where(owner == token, 1.0, 0.0).astype(BF16)
    last = dot(weight_ref[...], other_ref[...], NT).astype(BF16)
    placed = dot(first_ref[...], order[:half], NN) + dot(last, order[half:], NN)
    out_ref[...] = placed.astype(BF16)


def project(me, weight_t, first, other):
    vmem = pl.BlockSpec(memory_space=pltpu.VMEM)
    return pl.pallas_call(
        project_kernel,
        out_shape=jax.ShapeDtypeStruct((COLS, TOKENS), BF16),
        in_specs=[pl.BlockSpec(memory_space=pltpu.SMEM), vmem, vmem, vmem],
        out_specs=vmem,
        compiler_params=pltpu.CompilerParams(vmem_limit_bytes=16 * 2**20),
        name="project",
    )(me, weight_t, first, other)


def dispatch_kernel(p0, p1, p2, p3, residual_ref, gain_ref, rank_ref, stream_ref, out_ref):
    attention = (p0[...].astype(F32) + p2[...].astype(F32)) + (
        p1[...].astype(F32) + p3[...].astype(F32)
    )
    stream = residual_ref[...].astype(F32) + attention
    stream_ref[...] = stream
    squares = jnp.sum(stream * stream, axis=0, keepdims=True)
    high = squares.astype(BF16).astype(F32)
    low = squares - high
    tail = lax.broadcasted_iota(jnp.int32, (ROWS - COLS, TOKENS), 0)
    tail = jnp.where(tail == 0, high, jnp.where(tail == 1, low, 0.0))
    scaled = (stream * gain_ref[...]).astype(BF16)
    rows = jnp.concatenate([scaled, tail.astype(BF16)], axis=0)
    for e in range(EXPERTS):
        chosen = slot_onehot(rank_ref[e : e + 1, :])
        out_ref[e] = dot(rows, chosen, NT).astype(BF16)


def dispatch(parts, residual_t, gain, rank):
    vmem = pl.BlockSpec(memory_space=pltpu.VMEM)
    return pl.pallas_call(
        dispatch_kernel,
        out_shape=(
            jax.ShapeDtypeStruct((COLS, TOKENS), F32),
            jax.ShapeDtypeStruct((EXPERTS, ROWS, SLOTS), BF16),
        ),
        in_specs=[vmem] * 7,
        out_specs=(vmem, vmem),
        compiler_params=pltpu.CompilerParams(vmem_limit_bytes=16 * 2**20),
        cost_estimate=pl.CostEstimate(
            flops=30_000_000_000, bytes_accessed=2 * EXPERTS * ROWS * SLOTS, transcendentals=0
        ),
        name="dispatch",
    )(*parts, residual_t, gain, rank)


def expert_kernel(slot_weight_ref, rows_ref, gate_ref, up_ref, down_ref, out_ref):
    width = gate_ref.shape[1]
    gate = jnp.zeros((SLOTS, width), F32)
    up = jnp.zeros((SLOTS, width), F32)
    parts = jnp.zeros((ROWS - COLS, SLOTS), F32)
    for j in range(EXPERTS):
        rows = rows_ref[j, :COLS, :]
        parts = parts + rows_ref[j, COLS:, :].astype(F32)
        gate = gate + dot(rows, gate_ref[j * COLS : (j + 1) * COLS, :], TN)
        up = up + dot(rows, up_ref[j * COLS : (j + 1) * COLS, :], TN)
    squares = jnp.sum(parts, axis=0, keepdims=True)
    factor = lax.rsqrt(squares / D + NORM_EPS)
    row = lax.broadcasted_iota(jnp.int32, (SLOTS, SLOTS), 0)
    column = lax.broadcasted_iota(jnp.int32, (SLOTS, SLOTS), 1)
    factor = jnp.sum(jnp.where(row == column, factor, 0.0), axis=1, keepdims=True)
    gate = gate * factor
    up = up * factor
    value = gate / (1.0 + jnp.exp(-gate)) * up
    hidden = (value * slot_weight_ref[:, :1]).astype(BF16)
    for j in range(EXPERTS // GROUP):
        result = dot(hidden, down_ref[:, j * GROUP * COLS : (j + 1) * GROUP * COLS], NN)
        out_ref[j * GROUP : (j + 1) * GROUP] = result.T.astype(BF16).reshape(GROUP, COLS, SLOTS)


def expert(slot_weight, rows, gate_weight, up_weight, down_weight):
    vmem = pl.BlockSpec(memory_space=pltpu.VMEM)
    return pl.pallas_call(
        expert_kernel,
        out_shape=jax.ShapeDtypeStruct((EXPERTS, COLS, SLOTS), BF16),
        in_specs=[vmem] * 5,
        out_specs=vmem,
        compiler_params=pltpu.CompilerParams(vmem_limit_bytes=32 * 2**20),
        name="expert",
    )(slot_weight, rows, gate_weight, up_weight, down_weight)


def combine_kernel(returned_ref, rank_ref, out_ref):
    total = jnp.zeros((COLS, TOKENS), F32)
    for e in range(EXPERTS):
        total = total + dot(returned_ref[e], slot_onehot(rank_ref[e : e + 1, :]), NN)
    out_ref[...] = total.astype(BF16)


def combine(returned, rank):
    vmem = pl.BlockSpec(memory_space=pltpu.VMEM)
    return pl.pallas_call(
        combine_kernel,
        out_shape=jax.ShapeDtypeStruct((COLS, TOKENS), BF16),
        in_specs=[vmem, vmem],
        out_specs=vmem,
        compiler_params=pltpu.CompilerParams(vmem_limit_bytes=16 * 2**20),
        name="combine",
    )(returned, rank)


def around_z(part):
    size = lax.axis_size("head")
    return [part] + [
        lax.ppermute(part, "head", [(z, (z + step) % size) for z in range(size)])
        for step in range(1, size)
    ]


def per_device(
    queries,
    latent_cache,
    lengths,
    value_up,
    output_weight,
    residual,
    norm_gain,
    expert_ids,
    expert_weight,
    gate_weight,
    up_weight,
    down_weight,
):
    local_seqs = queries.shape[0]
    me = lax.axis_index("ep").astype(jnp.int32).reshape(1)
    values = attend(lengths, queries, latent_cache.swapaxes(1, 2), value_up)

    chips = EXPERTS // 2
    same_core = [[2 * chip + core for chip in range(chips)] for core in range(2)]
    copies = jnp.broadcast_to(values[None], (chips,) + values.shape)
    mine = lax.all_to_all(
        copies, "ep", split_axis=0, concat_axis=0, tiled=True, axis_index_groups=same_core
    ).reshape(chips * local_seqs, -1)
    other = lax.ppermute(mine, "ep", [(i, i ^ 1) for i in range(EXPERTS)])
    first = project_half(output_weight.T, mine)
    rank, slot_weight = route(me, expert_ids.T, expert_weight.T)
    first, rank, slot_weight = lax.optimization_barrier((first, rank, slot_weight))
    partial = project(me, output_weight.T, first, other)

    stream, outgoing = dispatch(around_z(partial), residual.T, norm_gain[:, None], rank)
    arrived = lax.all_to_all(outgoing, "ep", split_axis=0, concat_axis=0, tiled=True)
    results = expert(slot_weight, arrived, gate_weight[0], up_weight[0], down_weight[0])
    returned = lax.all_to_all(results, "ep", split_axis=0, concat_axis=0, tiled=True)
    c0, c1, c2, c3 = around_z(combine(returned, rank))
    combined = (c0.astype(F32) + c2.astype(F32)) + (c1.astype(F32) + c3.astype(F32))
    return (stream + combined).astype(BF16).T


def solution(mesh):
    placed = (
        P("ep", "head", None),
        P("ep", None, None),
        P("ep"),
        P("head", None, None),
        P("head", "ep"),
        P(None, "ep"),
        P("ep"),
        P(),
        P(),
        P("ep", None, "head"),
        P("ep", None, "head"),
        P("ep", "head", None),
    )
    return jax.shard_map(
        per_device, mesh=mesh, in_specs=placed, out_specs=P(None, "ep"), check_vma=False
    )
```

time: 141 us -> 128 us (0.908)
  matrix products: 14.4 us -> 0 us
  Pallas kernels: 12.5 us -> 18.7 us
  local copies, waits for them, and re-layouts: 5.31 us -> 1.23 us
    dot_general x3 -> x0, matrix products: 14.4 us -> none  [the longest x1 6.01 us: per_device(): jnp.einsum('shc,scl->shl', attn_weights, latent_cache[:, :, :latent_width...]
    pallas_call x1 -> x3, Pallas kernels: 6.06 us -> 12.7 us  [the longest x1 9.95 us: attend(): pl.pallas_call(attend_kernel, grid=(seqs // SEQS,), out_shape=jax.ShapeDt...]
    unnamed x20 -> x16, local copies, waits for them, and re-layouts: 5.08 us -> 0.04 us
    ppermute x1, waiting for transfers between devices: 2.42 us -> 0.18 us  [per_device(): other = lax.ppermute(mine, 'ep', [(i, i ^ 1) for i in range(EXPERTS)])]
    ppermute x6, waiting for transfers between devices: 10.8 us -> 12.4 us  [around_z(): lax.ppermute(part, 'head', [(z, (z + step) % size) for z in range(size)])]
  transfers between devices with their start and end apart: 7 -> 7, of which waited for: 7 -> 7; matrix products, arithmetic and copies ran while one was open for 0% -> 0% of each run, Pallas kernels for 1% -> 2%
where the time goes in v2:
time: 128 us; the launch traced here: 126 us
  blocking collectives  83.7 us (65%)
  Pallas kernels  18.7 us (15%)
  waiting for transfers between devices  12.6 us (10%)
  starting transfers between devices  8.46 us (7%)
    all_to_all x1, blocking collectives, per_device(): lax.all_to_all(outgoing, 'ep', split_axis=0, concat_axis=0, tiled=True)  31.1 us
    all_to_all x1, blocking collectives, per_device(): lax.all_to_all(results, 'ep', split_axis=0, concat_axis=0, tiled=True)  29 us
    all_to_all x1, blocking collectives, per_device(): lax.all_to_all(copies, 'ep', split_axis=0, concat_axis=0, tiled=True, axi...  23.6 us
    ppermute x6, waiting for transfers between devices, around_z(): lax.ppermute(part, 'head', [(z, (z + step) % size) for z in range(size)])  12.4 us
    pallas_call x1, Pallas kernels, attend(): pl.pallas_call(attend_kernel, grid=(seqs // SEQS,), out_shape=jax.ShapeDt...  9.95 us
    ppermute x6, starting transfers between devices, around_z(): lax.ppermute(part, 'head', [(z, (z + step) % size) for z in range(size)])  6.47 us
  transfers between devices with their start and end apart: 7, of which 7 were waited for; matrix products, arithmetic and copies ran while one was open for 0% of the time, Pallas kernels for 2%

profile of v2, /device:TPU:1, one launch (start us, length us, event | category | flops | bytes accessed | tf_op | source)
XLA Modules:
  0.0 125.5 jit_solution(8532032288532393634)
XLA Ops:
  0.0 9.9 %attend.1 = bf16[8,4096]{1,0:T(8,128)(2,1)} custom-call(s32[8]{0:T(128)} %lengths_ref.1, bf16[8,32,576]{2,1,0:T(8,128)(2,1)} %queries_ref.1, bf16[8,576,1024]{2,1,0:T(8,128)(2,1)} %bitcast.21, bf16[32,512,128]{2,1,0:T(8,128)(2,1)} %up_hbm.1), custom_call_target="tpu_custom_call" | custom-call | tf_op jit(solution)/shard_map/attend/pallas_call | solution.py:63
  10.0 1.1 broadcast_in_dim.4
  11.1 23.6 %all_to_all.15 = bf16[16,8,4096]{2,1,0:T(8,128)(2,1)S(1)} all-to-all(bf16[16,8,4096]{2,1,0:T(8,128)(2,1)S(1)} %broadcast_in_dim.4), channel_id=1, replica_groups={{0,8,16,24,32,40,48,56,64,72,80,88,96,104,112,120},{4,12,20,28,36,44,52..., dimensions={0} | all-to-all | bytes 2097152 | tf_op jit(solution)/shard_map/all_to_all | solution.py:290
  34.7 2.0 %collective-permute-start = (bf16[128,4096]{1,0:T(8,128)(2,1)S(1)}, bf16[128,4096]{1,0:T(8,128)(2,1)}, u32[]{:S(2)}, u32[]{:S(2)}) collective-permute-start(bf16[128,4096]{1,0:T(8,128)(2,1)S(1)} %bitcast.15), channel_id=1, source_target_pairs={{0,4},{4,0},{8,12},{12,8},{16,20},{20,16},{24,28},{28,24},{32,36},... | collective-permute-start | bytes 3145736 | tf_op jit(solution)/shard_map/ppermute | solution.py:293
  36.7 1.6 %route.1 = (f32[32,256]{1,0:T(8,128)}, f32[128,128]{1,0:T(8,128)}) custom-call(s32[1]{0:T(128)} %bitcast.me_ref, s32[8,256]{1,0:T(8,128)} %bitcast.22, f32[8,256]{1,0:T(8,128)} %bitcast.23), custom_call_target="tpu_custom_call" | custom-call | tf_op jit(solution)/shard_map/route/pallas_call | solution.py:114
  38.3 0.6 project_half.1.first_ref
  39.1 2.1 %project.1.p0 = bf16[224,256]{1,0:T(8,128)(2,1)S(1)} custom-call(s32[1]{0:T(128)} %bitcast.me_ref, bf16[224,4096]{1,0:T(8,128)(2,1)S(1)} %bitcast.14, bf16[224,128]{1,0:T(8,128)(2,1)S(1)} %project_half.1.first_ref, bf16[128,4096]{1,0:T(8,128)(2,1)} %collective-permute-done.other_ref), custom_call_target="tpu_custom_call" | custom-call | tf_op jit(solution)/shard_map/project/pallas_call | solution.py:160
  41.2 3.8 %collective-permute-start.3 = (bf16[224,256]{1,0:T(8,128)(2,1)S(1)}, bf16[224,256]{1,0:T(8,128)(2,1)S(1)}, u32[]{:S(2)}, u32[]{:S(2)}) collective-permute-start(bf16[224,256]{1,0:T(8,128)(2,1)S(1)} %project.1.p0), channel_id=1, source_target_pairs={{0,3},{1,0},{2,1},{3,2},{4,7},{5,4},{6,5},{7,6},{8,11},{9,8},{10,9... | collective-permute-start | bytes 344072 | tf_op jit(solution)/shard_map/ppermute | solution.py:264
  45.0 0.7 collective-permute-start.1
  45.9 4.1 %collective-permute-done.3.p3 = bf16[224,256]{1,0:T(8,128)(2,1)S(1)} collective-permute-done((bf16[224,256]{1,0:T(8,128)(2,1)S(1)}, bf16[224,256]{1,0:T(8,128)(2,1)S(1)}, u32[]{:S(2)}, u32[]{:S(2)}) %collective-permute-start.3) | collective-permute-done | bytes 114720 | tf_op jit(solution)/shard_map/ppermute | solution.py:264
  50.0 0.7 collective-permute-done.2.p2
  50.7 2.8 %collective-permute-done.1.p1 = bf16[224,256]{1,0:T(8,128)(2,1)S(1)} collective-permute-done((bf16[224,256]{1,0:T(8,128)(2,1)S(1)}, bf16[224,256]{1,0:T(8,128)(2,1)S(1)}, u32[]{:S(2)}, u32[]{:S(2)}) %collective-permute-start.1) | collective-permute-done | bytes 114720 | tf_op jit(solution)/shard_map/ppermute | solution.py:264
  53.5 1.2 dispatch.1
  54.8 31.1 %all_to_all.16.rows_ref = bf16[32,240,128]{2,1,0:T(8,128)(2,1)S(1)} all-to-all(bf16[32,240,128]{2,1,0:T(8,128)(2,1)S(1)} %get-tuple-element.18), channel_id=1, replica_groups=mesh['ep'=32,'head'=4] {'ep'}, dimensions={0} | all-to-all | bytes 3932160 | tf_op jit(solution)/shard_map/all_to_all | solution.py:300
  85.8 2.1 %expert.1 = bf16[32,224,128]{2,1,0:T(8,128)(2,1)S(1)} custom-call(f32[128,128]{1,0:T(8,128)S(1)} %copy-done.4, bf16[32,240,128]{2,1,0:T(8,128)(2,1)S(1)} %all_to_all.16.rows_ref, bf16[7168,256]{1,0:T(8,128)(2,1)S(1)} %bitcast.17, bf16[7168,256]{1,0:T(8,128)(2,1)S(1)} %bitcast.18, bf16[256,7168]{1,0:T(8,128)(2,1)S(1)} %bitcast.19), custom_call_target="tpu_custom_call" | custom-call | tf_op jit(solution)/shard_map/expert/pallas_call | solution.py:232
  87.9 29.0 %all_to_all.17.returned_ref = bf16[32,224,128]{2,1,0:T(8,128)(2,1)S(1)} all-to-all(bf16[32,224,128]{2,1,0:T(8,128)(2,1)S(1)} %expert.1), channel_id=1, replica_groups=mesh['ep'=32,'head'=4] {'ep'}, dimensions={0} | all-to-all | bytes 3670016 | tf_op jit(solution)/shard_map/all_to_all | solution.py:302
  116.9 1.1 combine.1
  118.0 0.7 collective-permute-start.6
  118.7 0.8 collective-permute-start.5
  119.6 0.4 collective-permute-start.4
  120.0 2.2 %collective-permute-done.6 = bf16[224,256]{1,0:T(8,128)(2,1)S(1)} collective-permute-done((bf16[224,256]{1,0:T(8,128)(2,1)S(1)}, bf16[224,256]{1,0:T(8,128)(2,1)S(1)}, u32[]{:S(2)}, u32[]{:S(2)}) %collective-permute-start.6) | collective-permute-done | bytes 114720 | tf_op jit(solution)/shard_map/ppermute | solution.py:264
  122.2 1.4 %collective-permute-done.5 = bf16[224,256]{1,0:T(8,128)(2,1)S(1)} collective-permute-done((bf16[224,256]{1,0:T(8,128)(2,1)S(1)}, bf16[224,256]{1,0:T(8,128)(2,1)S(1)}, u32[]{:S(2)}, u32[]{:S(2)}) %collective-permute-start.5) | collective-permute-done | bytes 114720 | tf_op jit(solution)/shard_map/ppermute | solution.py:264
  123.6 1.2 collective-permute-done.4
  124.8 0.7 fusion
  (19 shorter events, 0.4 us)
Async XLA Ops:
  10.0 28.3 %copy-start = (bf16[4096,224]{0,1:T(8,128)(2,1)S(1)}, bf16[4096,224]{0,1:T(8,128)(2,1)}, u32[]{:S(2)}) copy-start(bf16[4096,224]{0,1:T(8,128)(2,1)} %param.16) | copy-start | bytes 5505028
  11.0 34.7 %copy-start.7 = (f32[224]{0:T(256)S(1)}, f32[224]{0:T(256)}, u32[]{:S(2)}) copy-start(f32[224]{0:T(256)} %param.18) | copy-start | bytes 2692
  11.1 42.4 %copy-start.6 = (bf16[256,224]{0,1:T(8,128)(2,1)S(1)}, bf16[256,224]{0,1:T(8,128)(2,1)}, u32[]{:S(2)}) copy-start(bf16[256,224]{0,1:T(8,128)(2,1)} %param.17) | copy-start | bytes 344068
  34.7 4.4 %collective-permute-start = (bf16[128,4096]{1,0:T(8,128)(2,1)S(1)}, bf16[128,4096]{1,0:T(8,128)(2,1)}, u32[]{:S(2)}, u32[]{:S(2)}) collective-permute-start(bf16[128,4096]{1,0:T(8,128)(2,1)S(1)} %bitcast.15), channel_id=1, source_target_pairs={{0,4},{4,0},{8,12},{12,8},{16,20},{20,16},{24,28},{28,24},{32,36},... | collective-permute-start | bytes 3145736 | tf_op jit(solution)/shard_map/ppermute | solution.py:293
  38.3 15.2 %copy-start.5 = (f32[32,256]{1,0:T(8,128)S(1)}, f32[32,256]{1,0:T(8,128)}, u32[]{:S(2)}) copy-start(f32[32,256]{1,0:T(8,128)} %get-tuple-element.15.rank_ref) | copy-start | bytes 98308
  41.2 8.8 %collective-permute-start.3 = (bf16[224,256]{1,0:T(8,128)(2,1)S(1)}, bf16[224,256]{1,0:T(8,128)(2,1)S(1)}, u32[]{:S(2)}, u32[]{:S(2)}) collective-permute-start(bf16[224,256]{1,0:T(8,128)(2,1)S(1)} %project.1.p0), channel_id=1, source_target_pairs={{0,3},{1,0},{2,1},{3,2},{4,7},{5,4},{6,5},{7,6},{8,11},{9,8},{10,9... | collective-permute-start | bytes 344072 | tf_op jit(solution)/shard_map/ppermute | solution.py:264
  45.0 5.6 %collective-permute-start.2 = (bf16[224,256]{1,0:T(8,128)(2,1)S(1)}, bf16[224,256]{1,0:T(8,128)(2,1)S(1)}, u32[]{:S(2)}, u32[]{:S(2)}) collective-permute-start(bf16[224,256]{1,0:T(8,128)(2,1)S(1)} %project.1.p0), channel_id=1, source_target_pairs={{0,2},{1,3},{2,0},{3,1},{4,6},{5,7},{6,4},{7,5},{8,10},{9,11},{10,... | collective-permute-start | bytes 344072 | tf_op jit(solution)/shard_map/ppermute | solution.py:264
  45.0 8.4 %collective-permute-start.1 = (bf16[224,256]{1,0:T(8,128)(2,1)S(1)}, bf16[224,256]{1,0:T(8,128)(2,1)S(1)}, u32[]{:S(2)}, u32[]{:S(2)}) collective-permute-start(bf16[224,256]{1,0:T(8,128)(2,1)S(1)} %project.1.p0), channel_id=1, source_target_pairs={{0,1},{1,2},{2,3},{3,0},{4,5},{5,6},{6,7},{7,4},{8,9},{9,10},{10,1... | collective-permute-start | bytes 344072 | tf_op jit(solution)/shard_map/ppermute | solution.py:264
  53.5 32.3 %copy-start.2 = (bf16[1,7168,256]{2,1,0:T(8,128)(2,1)S(1)}, bf16[1,7168,256]{2,1,0:T(8,128)(2,1)}, u32[]{:S(2)}) copy-start(bf16[1,7168,256]{2,1,0:T(8,128)(2,1)} %param.22) | copy-start | bytes 11010052
  53.5 32.3 %copy-start.3 = (bf16[1,256,7168]{2,1,0:T(8,128)(2,1)S(1)}, bf16[1,256,7168]{2,1,0:T(8,128)(2,1)}, u32[]{:S(2)}) copy-start(bf16[1,256,7168]{2,1,0:T(8,128)(2,1)} %param.23) | copy-start | bytes 11010052
  54.7 31.1 %copy-start.1 = (bf16[1,7168,256]{2,1,0:T(8,128)(2,1)S(1)}, bf16[1,7168,256]{2,1,0:T(8,128)(2,1)}, u32[]{:S(2)}) copy-start(bf16[1,7168,256]{2,1,0:T(8,128)(2,1)} %param.21) | copy-start | bytes 11010052
  54.7 31.1 %copy-start.4 = (f32[128,128]{1,0:T(8,128)S(1)}, f32[128,128]{1,0:T(8,128)}, u32[]{:S(2)}) copy-start(f32[128,128]{1,0:T(8,128)} %get-tuple-element.17.slot_weight_ref) | copy-start | bytes 196612
  118.0 4.2 %collective-permute-start.6 = (bf16[224,256]{1,0:T(8,128)(2,1)S(1)}, bf16[224,256]{1,0:T(8,128)(2,1)S(1)}, u32[]{:S(2)}, u32[]{:S(2)}) collective-permute-start(bf16[224,256]{1,0:T(8,128)(2,1)S(1)} %combine.1), channel_id=1, source_target_pairs={{0,3},{1,0},{2,1},{3,2},{4,7},{5,4},{6,5},{7,6},{8,11},{9,8},{10,9... | collective-permute-start | bytes 344072 | tf_op jit(solution)/shard_map/ppermute | solution.py:264
  118.7 4.9 %collective-permute-start.5 = (bf16[224,256]{1,0:T(8,128)(2,1)S(1)}, bf16[224,256]{1,0:T(8,128)(2,1)S(1)}, u32[]{:S(2)}, u32[]{:S(2)}) collective-permute-start(bf16[224,256]{1,0:T(8,128)(2,1)S(1)} %combine.1), channel_id=1, source_target_pairs={{0,1},{1,2},{2,3},{3,0},{4,5},{5,6},{6,7},{7,4},{8,9},{9,10},{10,1... | collective-permute-start | bytes 344072 | tf_op jit(solution)/shard_map/ppermute | solution.py:264
  119.6 5.3 %collective-permute-start.4 = (bf16[224,256]{1,0:T(8,128)(2,1)S(1)}, bf16[224,256]{1,0:T(8,128)(2,1)S(1)}, u32[]{:S(2)}, u32[]{:S(2)}) collective-permute-start(bf16[224,256]{1,0:T(8,128)(2,1)S(1)} %combine.1), channel_id=1, source_target_pairs={{0,2},{1,3},{2,0},{3,1},{4,6},{5,7},{6,4},{7,5},{8,10},{9,11},{10,... | collective-permute-start | bytes 344072 | tf_op jit(solution)/shard_map/ppermute | solution.py:264

commit v3 on v2

--- a/solution.py
+++ b/solution.py
@@ -16,7 +16,8 @@
 ROWS = 240
 GROUP = 4
 TOPK = 8
-SEQS = 2
+PACKED = 16
+SEQS = 4
 
 BF16 = jnp.bfloat16
 F32 = jnp.float32
@@ -30,9 +31,12 @@
     return lax.dot_general(a, b, dims, preferred_element_type=F32)
 
 
-def attend_kernel(lengths_ref, queries_ref, cache_ref, up_hbm, out_ref, contexts, up_ref, up_sem):
+def attend_kernel(
+    lengths_ref, queries_ref, cache_ref, up_hbm, out_ref, contexts, up_ref, scores, probs, up_sem
+):
     step = pl.program_id(0)
     heads, latent, width = up_ref.shape
+    context = cache_ref.shape[2]
     up_copy = pltpu.make_async_copy(up_hbm, up_ref, up_sem)
 
     @pl.when(step == 0)
@@ -40,43 +44,51 @@
         up_copy.start()
 
     for b in range(SEQS):
+        scores[b] = dot(queries_ref[b], cache_ref[b], NN)
+    for b in range(SEQS):
         seq = step * SEQS + b
-        scores = dot(queries_ref[b], cache_ref[b], NN) * SCORE_SCALE
-        positions = lax.broadcasted_iota(jnp.int32, scores.shape, 1)
-        scores = jnp.where(positions < lengths_ref[seq], scores, -1e30)
-        exponents = jnp.exp(scores - jnp.max(scores, axis=1, keepdims=True))
-        probs = (exponents / jnp.sum(exponents, axis=1, keepdims=True)).astype(BF16)
-        contexts[seq] = dot(probs, cache_ref[b, :latent, :], NT)
+        positions = lax.broadcasted_iota(jnp.int32, (PACKED, context), 1)
+        allowed = positions < lengths_ref[seq]
+        for r in range(0, heads, PACKED):
+            part = jnp.where(allowed, scores[b, r : r + PACKED] * SCORE_SCALE, -1e30)
+            exponents = jnp.exp(part - jnp.max(part, axis=1, keepdims=True))
+            total = jnp.sum(exponents, axis=1, keepdims=True)
+            probs[b, r : r + PACKED] = (exponents / total).astype(BF16)
+        contexts[seq] = dot(probs[b], cache_ref[b, :latent, :], NT)
 
     @pl.when(step == pl.num_programs(0) - 1)
     def _():
         up_copy.wait()
         for h in range(heads):
             rows = contexts[:, h, :].astype(BF16)
-            out_ref[:, h * width : (h + 1) * width] = dot(rows, up_ref[h], NN).astype(BF16)
-
-
-def attend(lengths, queries, cache_t, value_up):
+            values = dot(rows, up_ref[h], NN).astype(BF16)
+            for copy in range(out_ref.shape[0]):
+                out_ref[copy, :, h * width : (h + 1) * width] = values
+
+
+def attend(lengths, queries, cache_t, value_up, copies):
     seqs, heads, kdim = queries.shape
     context = cache_t.shape[2]
     _, latent, width = value_up.shape
     return pl.pallas_call(
         attend_kernel,
         grid=(seqs // SEQS,),
-        out_shape=jax.ShapeDtypeStruct((seqs, heads * width), BF16),
+        out_shape=jax.ShapeDtypeStruct((copies, seqs, heads * width), BF16),
         in_specs=[
             pl.BlockSpec(memory_space=pltpu.SMEM),
             pl.BlockSpec((SEQS, heads, kdim), lambda i: (i, 0, 0)),
             pl.BlockSpec((SEQS, kdim, context), lambda i: (i, 0, 0)),
             pl.BlockSpec(memory_space=pl.ANY),
         ],
-        out_specs=pl.BlockSpec((seqs, heads * width), lambda i: (0, 0)),
+        out_specs=pl.BlockSpec((copies, seqs, heads * width), lambda i: (0, 0, 0)),
         scratch_shapes=[
             pltpu.VMEM((seqs, heads, latent), F32),
             pltpu.VMEM(value_up.shape, BF16),
+            pltpu.VMEM((SEQS, heads, context), F32),
+            pltpu.VMEM((SEQS, heads, context), BF16),
             pltpu.SemaphoreType.DMA,
         ],
-        compiler_params=pltpu.CompilerParams(vmem_limit_bytes=61 * 2**20),
+        compiler_params=pltpu.CompilerParams(vmem_limit_bytes=63 * 2**20),
         name="attend",
     )(lengths, queries, cache_t, value_up)
 
@@ -86,7 +98,10 @@
     return jnp.where(slots == rank_row, 1.0, 0.0).astype(BF16)
 
 
-def route_kernel(me_ref, ids_ref, weight_ref, rank_ref, slot_weight_ref, token_weight):
+def route_kernel(
+    me_ref, ids_ref, weight_ref, residual_ref, rank_ref, slot_weight_ref, residual_out, order_ref,
+    token_rank, token_weight,
+):
     experts = lax.broadcasted_iota(jnp.int32, (EXPERTS, TOKENS), 0)
     member = jnp.zeros((EXPERTS, TOKENS), F32)
     weight = jnp.zeros((EXPERTS, TOKENS), F32)
@@ -94,34 +109,46 @@
         hit = experts == ids_ref[k : k + 1, :]
         member = jnp.where(hit, 1.0, member)
         weight = jnp.where(hit, weight_ref[k : k + 1, :], weight)
-    before = lax.broadcasted_iota(jnp.int32, (TOKENS, TOKENS), 0)
-    after = lax.broadcasted_iota(jnp.int32, (TOKENS, TOKENS), 1)
-    earlier = jnp.where(before < after, 1.0, 0.0).astype(BF16)
-    rank = dot(member.astype(BF16), earlier, NN)
-    rank_ref[...] = jnp.where(member > 0.0, rank, -1.0)
+    row = lax.broadcasted_iota(jnp.int32, (TOKENS, TOKENS), 0)
+    column = lax.broadcasted_iota(jnp.int32, (TOKENS, TOKENS), 1)
+    earlier = jnp.where(row < column, 1.0, 0.0).astype(BF16)
+    rank = jnp.where(member > 0.0, dot(member.astype(BF16), earlier, NN), -1.0)
+    token_rank[...] = rank
     token_weight[...] = weight
     me = me_ref[0]
     slots = lax.broadcasted_iota(jnp.int32, (SLOTS, TOKENS), 0).astype(F32)
-    mine = slots == rank_ref[pl.ds(me, 1), :]
+    mine = slots == token_rank[pl.ds(me, 1), :]
     held = jnp.where(mine, token_weight[pl.ds(me, 1), :], 0.0)
     slot_weight_ref[...] = jnp.broadcast_to(
         jnp.sum(held, axis=1, keepdims=True), (SLOTS, 128)
     )
-
-
-def route(me, ids_t, weight_t):
+    core = lax.rem(me, 2)
+    second = (column >= TOKENS // 2).astype(jnp.int32)
+    within = column - second * (TOKENS // 2)
+    parity = jnp.where(second == 1, 1 - core, core)
+    token = ((within >> 3) * 2 + parity) * 8 + (within & 7)
+    order = jnp.where(row == token, 1.0, 0.0).astype(BF16)
+    order_ref[...] = order
+    rank_ref[...] = dot(rank.astype(BF16), order, NN)
+    residual_out[...] = dot(residual_ref[...], order, NN).astype(BF16)
+
+
+def route(me, ids_t, weight_t, residual_t):
     vmem = pl.BlockSpec(memory_space=pltpu.VMEM)
     return pl.pallas_call(
         route_kernel,
         out_shape=(
             jax.ShapeDtypeStruct((EXPERTS, TOKENS), F32),
             jax.ShapeDtypeStruct((SLOTS, 128), F32),
+            jax.ShapeDtypeStruct((COLS, TOKENS), BF16),
+            jax.ShapeDtypeStruct((TOKENS, TOKENS), BF16),
         ),
-        in_specs=[pl.BlockSpec(memory_space=pltpu.SMEM), vmem, vmem],
-        out_specs=(vmem, vmem),
-        scratch_shapes=[pltpu.VMEM((EXPERTS, TOKENS), F32)],
+        in_specs=[pl.BlockSpec(memory_space=pltpu.SMEM), vmem, vmem, vmem],
+        out_specs=(vmem,) * 4,
+        scratch_shapes=[pltpu.VMEM((EXPERTS, TOKENS), F32), pltpu.VMEM((EXPERTS, TOKENS), F32)],
+        compiler_params=pltpu.CompilerParams(vmem_limit_bytes=8 * 2**20),
         name="route",
-    )(me, ids_t, weight_t)
+    )(me, ids_t, weight_t, residual_t)
 
 
 def half_kernel(weight_ref, values_ref, out_ref):
@@ -140,31 +167,22 @@
     )(weight_t, values)
 
 
-def project_kernel(me_ref, weight_ref, first_ref, other_ref, out_ref):
-    core = lax.rem(me_ref[0], 2)
-    half = TOKENS // 2
-    column = lax.broadcasted_iota(jnp.int32, (TOKENS, TOKENS), 0)
-    token = lax.broadcasted_iota(jnp.int32, (TOKENS, TOKENS), 1)
-    second = (column >= half).astype(jnp.int32)
-    within = column - second * half
-    parity = jnp.where(second == 1, 1 - core, core)
-    owner = ((within >> 3) * 2 + parity) * 8 + (within & 7)
-    order = jnp.where(owner == token, 1.0, 0.0).astype(BF16)
-    last = dot(weight_ref[...], other_ref[...], NT).astype(BF16)
-    placed = dot(first_ref[...], order[:half], NN) + dot(last, order[half:], NN)
-    out_ref[...] = placed.astype(BF16)
-
-
-def project(me, weight_t, first, other):
+def project_kernel(weight_ref, first_ref, other_ref, out_ref):
+    half = other_ref.shape[0]
+    out_ref[:, :half] = first_ref[...]
+    out_ref[:, half:] = dot(weight_ref[...], other_ref[...], NT).astype(BF16)
+
+
+def project(weight_t, first, other):
     vmem = pl.BlockSpec(memory_space=pltpu.VMEM)
     return pl.pallas_call(
         project_kernel,
         out_shape=jax.ShapeDtypeStruct((COLS, TOKENS), BF16),
-        in_specs=[pl.BlockSpec(memory_space=pltpu.SMEM), vmem, vmem, vmem],
+        in_specs=[vmem, vmem, vmem],
         out_specs=vmem,
         compiler_params=pltpu.CompilerParams(vmem_limit_bytes=16 * 2**20),
         name="project",
-    )(me, weight_t, first, other)
+    )(weight_t, first, other)
 
 
 def dispatch_kernel(p0, p1, p2, p3, residual_ref, gain_ref, rank_ref, stream_ref, out_ref):
@@ -258,6 +276,26 @@
     )(returned, rank)
 
 
+def finish_kernel(stream_ref, c0, c1, c2, c3, order_ref, out_ref):
+    combined = (c0[...].astype(F32) + c2[...].astype(F32)) + (
+        c1[...].astype(F32) + c3[...].astype(F32)
+    )
+    mixed = (stream_ref[...] + combined).astype(BF16)
+    out_ref[...] = dot(mixed, order_ref[...], NT).astype(BF16)
+
+
+def finish(stream, parts, order):
+    vmem = pl.BlockSpec(memory_space=pltpu.VMEM)
+    return pl.pallas_call(
+        finish_kernel,
+        out_shape=jax.ShapeDtypeStruct((COLS, TOKENS), BF16),
+        in_specs=[vmem] * 6,
+        out_specs=vmem,
+        compiler_params=pltpu.CompilerParams(vmem_limit_bytes=16 * 2**20),
+        name="finish",
+    )(stream, *parts, order)
+
+
 def around_z(part):
     size = lax.axis_size("head")
     return [part] + [
@@ -282,27 +320,25 @@
 ):
     local_seqs = queries.shape[0]
     me = lax.axis_index("ep").astype(jnp.int32).reshape(1)
-    values = attend(lengths, queries, latent_cache.swapaxes(1, 2), value_up)
-
     chips = EXPERTS // 2
     same_core = [[2 * chip + core for chip in range(chips)] for core in range(2)]
-    copies = jnp.broadcast_to(values[None], (chips,) + values.shape)
+    copies = attend(lengths, queries, latent_cache.swapaxes(1, 2), value_up, chips)
+    weight_t = output_weight.T
     mine = lax.all_to_all(
         copies, "ep", split_axis=0, concat_axis=0, tiled=True, axis_index_groups=same_core
     ).reshape(chips * local_seqs, -1)
     other = lax.ppermute(mine, "ep", [(i, i ^ 1) for i in range(EXPERTS)])
-    first = project_half(output_weight.T, mine)
-    rank, slot_weight = route(me, expert_ids.T, expert_weight.T)
-    first, rank, slot_weight = lax.optimization_barrier((first, rank, slot_weight))
-    partial = project(me, output_weight.T, first, other)
-
-    stream, outgoing = dispatch(around_z(partial), residual.T, norm_gain[:, None], rank)
+    first = project_half(weight_t, mine)
+    partial = project(weight_t, first, other)
+    rank, slot_weight, residual_t, order = route(
+        me, expert_ids.T, expert_weight.T, residual.T
+    )
+
+    stream, outgoing = dispatch(around_z(partial), residual_t, norm_gain[:, None], rank)
     arrived = lax.all_to_all(outgoing, "ep", split_axis=0, concat_axis=0, tiled=True)
     results = expert(slot_weight, arrived, gate_weight[0], up_weight[0], down_weight[0])
     returned = lax.all_to_all(results, "ep", split_axis=0, concat_axis=0, tiled=True)
-    c0, c1, c2, c3 = around_z(combine(returned, rank))
-    combined = (c0.astype(F32) + c2.astype(F32)) + (c1.astype(F32) + c3.astype(F32))
-    return (stream + combined).astype(BF16).T
+    return finish(stream, around_z(combine(returned, rank)), order).T
 
 
 def solution(mesh):

time: 128 us -> 125 us (0.977); the launches traced: 126 us -> 125 us
  Pallas kernels: 18.7 us -> 15.5 us
  waiting for transfers between devices: 12.6 us -> 15.5 us
    ppermute x6, waiting for transfers between devices: 12.4 us -> 15.4 us  [around_z(): lax.ppermute(part, 'head', [(z, (z + step) % size) for z in range(size)])]
    unnamed x16, local copies, waits for them, and re-layouts: 0.04 us -> 1.54 us
    pallas_call x1, Pallas kernels: 2.09 us -> 0.63 us  [project(): pl.pallas_call(project_kernel, out_shape=jax.ShapeDtypeStruct((COLS, TOKE...]
    pallas_call x1, Pallas kernels: 9.95 us -> 8.63 us  [attend(): pl.pallas_call(attend_kernel, grid=(seqs // SEQS,), out_shape=jax.ShapeDt...]
    pallas_call x1, Pallas kernels: 1.59 us -> 0.27 us  [route(): pl.pallas_call(route_kernel, out_shape=(jax.ShapeDtypeStruct((EXPERTS, TO...]
  transfers between devices with their start and end apart: 7 -> 7, of which waited for: 7 -> 7; matrix products, arithmetic and copies ran while one was open for 0% -> 0% of each run, Pallas kernels for 2% -> 1%
where the time goes in v3:
time: 125 us
  blocking collectives  83.9 us (67%)
  Pallas kernels  15.5 us (12%)
  waiting for transfers between devices  15.5 us (12%)
  starting transfers between devices  8.05 us (6%)
  local copies, waits for them, and re-layouts  1.66 us (1%)
    all_to_all x1, blocking collectives, per_device(): lax.all_to_all(outgoing, 'ep', split_axis=0, concat_axis=0, tiled=True)  31.1 us
    all_to_all x1, blocking collectives, per_device(): lax.all_to_all(results, 'ep', split_axis=0, concat_axis=0, tiled=True)  29 us
    all_to_all x1, blocking collectives, per_device(): lax.all_to_all(copies, 'ep', split_axis=0, concat_axis=0, tiled=True, axi...  23.9 us
    ppermute x6, waiting for transfers between devices, around_z(): lax.ppermute(part, 'head', [(z, (z + step) % size) for z in range(size)])  15.4 us
    pallas_call x1, Pallas kernels, attend(): pl.pallas_call(attend_kernel, grid=(seqs // SEQS,), out_shape=jax.ShapeDt...  8.63 us
    ppermute x6, starting transfers between devices, around_z(): lax.ppermute(part, 'head', [(z, (z + step) % size) for z in range(size)])  6.07 us
  transfers between devices with their start and end apart: 7, of which 7 were waited for; matrix products, arithmetic and copies ran while one was open for 0% of the time, Pallas kernels for 1%

profile of v3, /device:TPU:1, one launch (start us, length us, event | category | flops | bytes accessed | tf_op | source)
XLA Modules:
  0.0 124.7 jit_solution(6082826470662218886)
XLA Ops:
  0.0 8.6 %attend.1 = bf16[16,8,4096]{2,1,0:T(8,128)(2,1)} custom-call(s32[8]{0:T(128)} %lengths_ref.1, bf16[8,32,576]{2,1,0:T(8,128)(2,1)} %queries_ref.1, bf16[8,576,1024]{2,1,0:T(8,128)(2,1)} %bitcast.22, bf16[32,512,128]{2,1,0:T(8,128)(2,1)} %up_hbm.1), custom_call_target="tpu_custom_call" | custom-call | tf_op jit(solution)/shard_map/attend/pallas_call | solution.py:73
  8.7 23.9 %all_to_all.15 = bf16[16,8,4096]{2,1,0:T(8,128)(2,1)S(1)} all-to-all(bf16[16,8,4096]{2,1,0:T(8,128)(2,1)} %attend.1), channel_id=1, replica_groups={{0,8,16,24,32,40,48,56,64,72,80,88,96,104,112,120},{4,12,20,28,36,44,52..., dimensions={0} | all-to-all | bytes 2097152 | tf_op jit(solution)/shard_map/all_to_all | solution.py:327
  32.5 2.0 %collective-permute-start = (bf16[128,4096]{1,0:T(8,128)(2,1)S(1)}, bf16[128,4096]{1,0:T(8,128)(2,1)S(1)}, u32[]{:S(2)}, u32[]{:S(2)}) collective-permute-start(bf16[128,4096]{1,0:T(8,128)(2,1)S(1)} %bitcast.14), channel_id=1, source_target_pairs={{0,4},{4,0},{8,12},{12,8},{16,20},{20,16},{24,28},{28,24},{32,36},... | collective-permute-start | bytes 3145736 | tf_op jit(solution)/shard_map/ppermute | solution.py:330
  34.5 1.5 %copy-done = bf16[4096,224]{0,1:T(8,128)(2,1)S(1)} copy-done((bf16[4096,224]{0,1:T(8,128)(2,1)S(1)}, bf16[4096,224]{0,1:T(8,128)(2,1)}, u32[]{:S(2)}) %copy-start) | copy-done | bytes 1835032
  36.0 0.6 project_half.1.first_ref
  36.7 0.1 collective-permute-done.other_ref
  36.8 0.6 project.1.p0
  37.5 3.8 %collective-permute-start.3 = (bf16[224,256]{1,0:T(8,128)(2,1)S(1)}, bf16[224,256]{1,0:T(8,128)(2,1)S(1)}, u32[]{:S(2)}, u32[]{:S(2)}) collective-permute-start(bf16[224,256]{1,0:T(8,128)(2,1)S(1)} %project.1.p0), channel_id=1, source_target_pairs={{0,3},{1,0},{2,1},{3,2},{4,7},{5,4},{6,5},{7,6},{8,11},{9,8},{10,9... | collective-permute-start | bytes 344072 | tf_op jit(solution)/shard_map/ppermute | solution.py:302
  41.3 0.7 collective-permute-start.1
  42.1 0.3 route.1
  42.4 3.8 %collective-permute-done.3.p3 = bf16[224,256]{1,0:T(8,128)(2,1)S(1)} collective-permute-done((bf16[224,256]{1,0:T(8,128)(2,1)S(1)}, bf16[224,256]{1,0:T(8,128)(2,1)S(1)}, u32[]{:S(2)}, u32[]{:S(2)}) %collective-permute-start.3) | collective-permute-done | bytes 114720 | tf_op jit(solution)/shard_map/ppermute | solution.py:302
  46.2 0.7 collective-permute-done.2.p2
  46.9 2.8 %collective-permute-done.1.p1 = bf16[224,256]{1,0:T(8,128)(2,1)S(1)} collective-permute-done((bf16[224,256]{1,0:T(8,128)(2,1)S(1)}, bf16[224,256]{1,0:T(8,128)(2,1)S(1)}, u32[]{:S(2)}, u32[]{:S(2)}) %collective-permute-start.1) | collective-permute-done | bytes 114720 | tf_op jit(solution)/shard_map/ppermute | solution.py:302
  49.7 1.2 dispatch.1
  51.0 31.1 %all_to_all.16.rows_ref = bf16[32,240,128]{2,1,0:T(8,128)(2,1)S(1)} all-to-all(bf16[32,240,128]{2,1,0:T(8,128)(2,1)S(1)} %get-tuple-element.15), channel_id=1, replica_groups=mesh['ep'=32,'head'=4] {'ep'}, dimensions={0} | all-to-all | bytes 3932160 | tf_op jit(solution)/shard_map/all_to_all | solution.py:338
  82.0 2.1 %expert.1 = bf16[32,224,128]{2,1,0:T(8,128)(2,1)S(1)} custom-call(f32[128,128]{1,0:T(8,128)S(1)} %get-tuple-element.14.slot_weight_ref, bf16[32,240,128]{2,1,0:T(8,128)(2,1)S(1)} %all_to_all.16.rows_ref, bf16[7168,256]{1,0:T(8,128)(2,1)S(1)} %bitcast.16, bf16[7168,256]{1,0:T(8,128)(2,1)S(1)} %bitcast.17, bf16[256,7168]{1,0:T(8,128)(2,1)S(1)} %bitcast.18), custom_call_target="tpu_custom_call" | custom-call | tf_op jit(solution)/shard_map/expert/pallas_call | solution.py:250
  84.1 29.0 %all_to_all.17.returned_ref = bf16[32,224,128]{2,1,0:T(8,128)(2,1)S(1)} all-to-all(bf16[32,224,128]{2,1,0:T(8,128)(2,1)S(1)} %expert.1), channel_id=1, replica_groups=mesh['ep'=32,'head'=4] {'ep'}, dimensions={0} | all-to-all | bytes 3670016 | tf_op jit(solution)/shard_map/all_to_all | solution.py:340
  113.1 1.1 combine.1.c0
  114.2 0.7 collective-permute-start.6
  114.9 0.8 collective-permute-start.4
  115.8 2.6 %collective-permute-done.6.c3 = bf16[224,256]{1,0:T(8,128)(2,1)S(1)} collective-permute-done((bf16[224,256]{1,0:T(8,128)(2,1)S(1)}, bf16[224,256]{1,0:T(8,128)(2,1)S(1)}, u32[]{:S(2)}, u32[]{:S(2)}) %collective-permute-start.6) | collective-permute-done | bytes 114720 | tf_op jit(solution)/shard_map/ppermute | solution.py:302
  118.4 1.8 %collective-permute-done.5.c2 = bf16[224,256]{1,0:T(8,128)(2,1)S(1)} collective-permute-done((bf16[224,256]{1,0:T(8,128)(2,1)S(1)}, bf16[224,256]{1,0:T(8,128)(2,1)S(1)}, u32[]{:S(2)}, u32[]{:S(2)}) %collective-permute-start.5) | collective-permute-done | bytes 114720 | tf_op jit(solution)/shard_map/ppermute | solution.py:302
  120.2 3.7 %collective-permute-done.4.c1 = bf16[224,256]{1,0:T(8,128)(2,1)S(1)} collective-permute-done((bf16[224,256]{1,0:T(8,128)(2,1)S(1)}, bf16[224,256]{1,0:T(8,128)(2,1)S(1)}, u32[]{:S(2)}, u32[]{:S(2)}) %collective-permute-start.4) | collective-permute-done | bytes 114720 | tf_op jit(solution)/shard_map/ppermute | solution.py:302
  123.8 0.9 finish.1
  (18 shorter events, 0.2 us)
Async XLA Ops:
  8.6 33.3 %copy-start.7 = (f32[224]{0:T(256)S(1)}, f32[224]{0:T(256)}, u32[]{:S(2)}) copy-start(f32[224]{0:T(256)} %param.18) | copy-start | bytes 2692
  8.6 33.5 %copy-start.4 = (bf16[256,224]{0,1:T(8,128)(2,1)S(1)}, bf16[256,224]{0,1:T(8,128)(2,1)}, u32[]{:S(2)}) copy-start(bf16[256,224]{0,1:T(8,128)(2,1)} %param.17) | copy-start | bytes 344068
  8.7 33.5 %copy-start.5 = (s32[256,8]{0,1:T(8,128)S(1)}, s32[256,8]{0,1:T(8,128)}, u32[]{:S(2)}) copy-start(s32[256,8]{0,1:T(8,128)} %param.19) | copy-start | bytes 24580
  8.7 33.5 %copy-start.6 = (f32[256,8]{0,1:T(8,128)S(1)}, f32[256,8]{0,1:T(8,128)}, u32[]{:S(2)}) copy-start(f32[256,8]{0,1:T(8,128)} %param.20) | copy-start | bytes 24580
  32.5 4.3 %collective-permute-start = (bf16[128,4096]{1,0:T(8,128)(2,1)S(1)}, bf16[128,4096]{1,0:T(8,128)(2,1)S(1)}, u32[]{:S(2)}, u32[]{:S(2)}) collective-permute-start(bf16[128,4096]{1,0:T(8,128)(2,1)S(1)} %bitcast.14), channel_id=1, source_target_pairs={{0,4},{4,0},{8,12},{12,8},{16,20},{20,16},{24,28},{28,24},{32,36},... | collective-permute-start | bytes 3145736 | tf_op jit(solution)/shard_map/ppermute | solution.py:330
  34.5 1.5 %copy-start = (bf16[4096,224]{0,1:T(8,128)(2,1)S(1)}, bf16[4096,224]{0,1:T(8,128)(2,1)}, u32[]{:S(2)}) copy-start(bf16[4096,224]{0,1:T(8,128)(2,1)} %param.16) | copy-start | bytes 5505028
  37.5 8.8 %collective-permute-start.3 = (bf16[224,256]{1,0:T(8,128)(2,1)S(1)}, bf16[224,256]{1,0:T(8,128)(2,1)S(1)}, u32[]{:S(2)}, u32[]{:S(2)}) collective-permute-start(bf16[224,256]{1,0:T(8,128)(2,1)S(1)} %project.1.p0), channel_id=1, source_target_pairs={{0,3},{1,0},{2,1},{3,2},{4,7},{5,4},{6,5},{7,6},{8,11},{9,8},{10,9... | collective-permute-start | bytes 344072 | tf_op jit(solution)/shard_map/ppermute | solution.py:302
  41.3 5.6 %collective-permute-start.2 = (bf16[224,256]{1,0:T(8,128)(2,1)S(1)}, bf16[224,256]{1,0:T(8,128)(2,1)S(1)}, u32[]{:S(2)}, u32[]{:S(2)}) collective-permute-start(bf16[224,256]{1,0:T(8,128)(2,1)S(1)} %project.1.p0), channel_id=1, source_target_pairs={{0,2},{1,3},{2,0},{3,1},{4,6},{5,7},{6,4},{7,5},{8,10},{9,11},{10,... | collective-permute-start | bytes 344072 | tf_op jit(solution)/shard_map/ppermute | solution.py:302
  41.3 8.4 %collective-permute-start.1 = (bf16[224,256]{1,0:T(8,128)(2,1)S(1)}, bf16[224,256]{1,0:T(8,128)(2,1)S(1)}, u32[]{:S(2)}, u32[]{:S(2)}) collective-permute-start(bf16[224,256]{1,0:T(8,128)(2,1)S(1)} %project.1.p0), channel_id=1, source_target_pairs={{0,1},{1,2},{2,3},{3,0},{4,5},{5,6},{6,7},{7,4},{8,9},{9,10},{10,1... | collective-permute-start | bytes 344072 | tf_op jit(solution)/shard_map/ppermute | solution.py:302
  49.7 32.3 %copy-start.2 = (bf16[1,7168,256]{2,1,0:T(8,128)(2,1)S(1)}, bf16[1,7168,256]{2,1,0:T(8,128)(2,1)}, u32[]{:S(2)}) copy-start(bf16[1,7168,256]{2,1,0:T(8,128)(2,1)} %param.22) | copy-start | bytes 11010052
  49.7 32.3 %copy-start.3 = (bf16[1,256,7168]{2,1,0:T(8,128)(2,1)S(1)}, bf16[1,256,7168]{2,1,0:T(8,128)(2,1)}, u32[]{:S(2)}) copy-start(bf16[1,256,7168]{2,1,0:T(8,128)(2,1)} %param.23) | copy-start | bytes 11010052
  51.0 31.1 %copy-start.1 = (bf16[1,7168,256]{2,1,0:T(8,128)(2,1)S(1)}, bf16[1,7168,256]{2,1,0:T(8,128)(2,1)}, u32[]{:S(2)}) copy-start(bf16[1,7168,256]{2,1,0:T(8,128)(2,1)} %param.21) | copy-start | bytes 11010052
  114.2 4.2 %collective-permute-start.6 = (bf16[224,256]{1,0:T(8,128)(2,1)S(1)}, bf16[224,256]{1,0:T(8,128)(2,1)S(1)}, u32[]{:S(2)}, u32[]{:S(2)}) collective-permute-start(bf16[224,256]{1,0:T(8,128)(2,1)S(1)} %combine.1.c0), channel_id=1, source_target_pairs={{0,3},{1,0},{2,1},{3,2},{4,7},{5,4},{6,5},{7,6},{8,11},{9,8},{10,9... | collective-permute-start | bytes 344072 | tf_op jit(solution)/shard_map/ppermute | solution.py:302
  114.9 5.3 %collective-permute-start.5 = (bf16[224,256]{1,0:T(8,128)(2,1)S(1)}, bf16[224,256]{1,0:T(8,128)(2,1)S(1)}, u32[]{:S(2)}, u32[]{:S(2)}) collective-permute-start(bf16[224,256]{1,0:T(8,128)(2,1)S(1)} %combine.1.c0), channel_id=1, source_target_pairs={{0,2},{1,3},{2,0},{3,1},{4,6},{5,7},{6,4},{7,5},{8,10},{9,11},{10,... | collective-permute-start | bytes 344072 | tf_op jit(solution)/shard_map/ppermute | solution.py:302
  114.9 8.9 %collective-permute-start.4 = (bf16[224,256]{1,0:T(8,128)(2,1)S(1)}, bf16[224,256]{1,0:T(8,128)(2,1)S(1)}, u32[]{:S(2)}, u32[]{:S(2)}) collective-permute-start(bf16[224,256]{1,0:T(8,128)(2,1)S(1)} %combine.1.c0), channel_id=1, source_target_pairs={{0,1},{1,2},{2,3},{3,0},{4,5},{5,6},{6,7},{7,4},{8,9},{9,10},{10,1... | collective-permute-start | bytes 344072 | tf_op jit(solution)/shard_map/ppermute | solution.py:302

commit v4 on v3

--- a/solution.py
+++ b/solution.py
@@ -13,7 +13,7 @@
 EXPERTS = 32
 SLOTS = 128
 COLS = 224
-ROWS = 240
+ROWS = 232
 GROUP = 4
 TOPK = 8
 PACKED = 16
@@ -93,9 +93,15 @@
     )(lengths, queries, cache_t, value_up)
 
 
-def slot_onehot(rank_row):
+def slot_onehot(rank_ref, first, count):
     slots = lax.broadcasted_iota(jnp.int32, (SLOTS, TOKENS), 0).astype(F32)
-    return jnp.where(slots == rank_row, 1.0, 0.0).astype(BF16)
+    return jnp.concatenate(
+        [
+            jnp.where(slots == rank_ref[e : e + 1, :], 1.0, 0.0).astype(BF16)
+            for e in range(first, first + count)
+        ],
+        axis=0,
+    )
 
 
 def route_kernel(
@@ -198,9 +204,10 @@
     tail = jnp.where(tail == 0, high, jnp.where(tail == 1, low, 0.0))
     scaled = (stream * gain_ref[...]).astype(BF16)
     rows = jnp.concatenate([scaled, tail.astype(BF16)], axis=0)
-    for e in range(EXPERTS):
-        chosen = slot_onehot(rank_ref[e : e + 1, :])
-        out_ref[e] = dot(rows, chosen, NT).astype(BF16)
+    for e in range(0, EXPERTS, 2):
+        picked = dot(rows, slot_onehot(rank_ref, e, 2), NT).astype(BF16)
+        out_ref[e] = picked[:, :SLOTS]
+        out_ref[e + 1] = picked[:, SLOTS:]
 
 
 def dispatch(parts, residual_t, gain, rank):
@@ -227,10 +234,11 @@
     up = jnp.zeros((SLOTS, width), F32)
     parts = jnp.zeros((ROWS - COLS, SLOTS), F32)
     for j in range(EXPERTS):
-        rows = rows_ref[j, :COLS, :]
         parts = parts + rows_ref[j, COLS:, :].astype(F32)
-        gate = gate + dot(rows, gate_ref[j * COLS : (j + 1) * COLS, :], TN)
-        up = up + dot(rows, up_ref[j * COLS : (j + 1) * COLS, :], TN)
+    for j in range(0, EXPERTS, GROUP):
+        rows = rows_ref[j : j + GROUP, :COLS, :].reshape(GROUP * COLS, SLOTS)
+        gate = gate + dot(rows, gate_ref[j * COLS : (j + GROUP) * COLS, :], TN)
+        up = up + dot(rows, up_ref[j * COLS : (j + GROUP) * COLS, :], TN)
     squares = jnp.sum(parts, axis=0, keepdims=True)
     factor = lax.rsqrt(squares / D + NORM_EPS)
     row = lax.broadcasted_iota(jnp.int32, (SLOTS, SLOTS), 0)
@@ -259,8 +267,9 @@
 
 def combine_kernel(returned_ref, rank_ref, out_ref):
     total = jnp.zeros((COLS, TOKENS), F32)
-    for e in range(EXPERTS):
-        total = total + dot(returned_ref[e], slot_onehot(rank_ref[e : e + 1, :]), NN)
+    for e in range(0, EXPERTS, GROUP):
+        rows = jnp.concatenate([returned_ref[e + i] for i in range(GROUP)], axis=1)
+        total = total + dot(rows, slot_onehot(rank_ref, e, GROUP), NN)
     out_ref[...] = total.astype(BF16)
 
 

time: 125 us -> 123 us (0.984)
  no operation moved by 1% of the time
where the time goes in v4:
time: 123 us
  blocking collectives  83.2 us (68%)
  waiting for transfers between devices  15.5 us (13%)
  Pallas kernels  14.6 us (12%)
  starting transfers between devices  8.05 us (7%)
  local copies, waits for them, and re-layouts  1.66 us (1%)
    all_to_all x1, blocking collectives, per_device(): lax.all_to_all(outgoing, 'ep', split_axis=0, concat_axis=0, tiled=True)  30.2 us
    all_to_all x1, blocking collectives, per_device(): lax.all_to_all(results, 'ep', split_axis=0, concat_axis=0, tiled=True)  29.2 us
    all_to_all x1, blocking collectives, per_device(): lax.all_to_all(copies, 'ep', split_axis=0, concat_axis=0, tiled=True, axi...  23.9 us
    ppermute x6, waiting for transfers between devices, around_z(): lax.ppermute(part, 'head', [(z, (z + step) % size) for z in range(size)])  15.4 us
    pallas_call x1, Pallas kernels, attend(): pl.pallas_call(attend_kernel, grid=(seqs // SEQS,), out_shape=jax.ShapeDt...  8.63 us
    ppermute x6, starting transfers between devices, around_z(): lax.ppermute(part, 'head', [(z, (z + step) % size) for z in range(size)])  6.07 us
  transfers between devices with their start and end apart: 7, of which 7 were waited for; matrix products, arithmetic and copies ran while one was open for 0% of the time, Pallas kernels for 1%

profile of v4, /device:TPU:1, one launch (start us, length us, event | category | flops | bytes accessed | tf_op | source)
XLA Modules:
  0.0 123.1 jit_solution(7547925912909532762)
XLA Ops:
  0.0 8.6 %attend.1 = bf16[16,8,4096]{2,1,0:T(8,128)(2,1)} custom-call(s32[8]{0:T(128)} %lengths_ref.1, bf16[8,32,576]{2,1,0:T(8,128)(2,1)} %queries_ref.1, bf16[8,576,1024]{2,1,0:T(8,128)(2,1)} %bitcast.22, bf16[32,512,128]{2,1,0:T(8,128)(2,1)} %up_hbm.1), custom_call_target="tpu_custom_call" | custom-call | tf_op jit(solution)/shard_map/attend/pallas_call | solution.py:73
  8.7 23.9 %all_to_all.15 = bf16[16,8,4096]{2,1,0:T(8,128)(2,1)S(1)} all-to-all(bf16[16,8,4096]{2,1,0:T(8,128)(2,1)} %attend.1), channel_id=1, replica_groups={{0,8,16,24,32,40,48,56,64,72,80,88,96,104,112,120},{4,12,20,28,36,44,52..., dimensions={0} | all-to-all | bytes 2097152 | tf_op jit(solution)/shard_map/all_to_all | solution.py:336
  32.5 2.0 %collective-permute-start = (bf16[128,4096]{1,0:T(8,128)(2,1)S(1)}, bf16[128,4096]{1,0:T(8,128)(2,1)S(1)}, u32[]{:S(2)}, u32[]{:S(2)}) collective-permute-start(bf16[128,4096]{1,0:T(8,128)(2,1)S(1)} %bitcast.14), channel_id=1, source_target_pairs={{0,4},{4,0},{8,12},{12,8},{16,20},{20,16},{24,28},{28,24},{32,36},... | collective-permute-start | bytes 3145736 | tf_op jit(solution)/shard_map/ppermute | solution.py:339
  34.5 1.5 %copy-done = bf16[4096,224]{0,1:T(8,128)(2,1)S(1)} copy-done((bf16[4096,224]{0,1:T(8,128)(2,1)S(1)}, bf16[4096,224]{0,1:T(8,128)(2,1)}, u32[]{:S(2)}) %copy-start) | copy-done | bytes 1835032
  36.0 0.6 project_half.1.first_ref
  36.7 0.1 collective-permute-done.other_ref
  36.8 0.6 project.1.p0
  37.5 3.8 %collective-permute-start.3 = (bf16[224,256]{1,0:T(8,128)(2,1)S(1)}, bf16[224,256]{1,0:T(8,128)(2,1)S(1)}, u32[]{:S(2)}, u32[]{:S(2)}) collective-permute-start(bf16[224,256]{1,0:T(8,128)(2,1)S(1)} %project.1.p0), channel_id=1, source_target_pairs={{0,3},{1,0},{2,1},{3,2},{4,7},{5,4},{6,5},{7,6},{8,11},{9,8},{10,9... | collective-permute-start | bytes 344072 | tf_op jit(solution)/shard_map/ppermute | solution.py:311
  41.3 0.7 collective-permute-start.1
  42.1 0.3 route.1
  42.4 3.8 %collective-permute-done.3.p3 = bf16[224,256]{1,0:T(8,128)(2,1)S(1)} collective-permute-done((bf16[224,256]{1,0:T(8,128)(2,1)S(1)}, bf16[224,256]{1,0:T(8,128)(2,1)S(1)}, u32[]{:S(2)}, u32[]{:S(2)}) %collective-permute-start.3) | collective-permute-done | bytes 114720 | tf_op jit(solution)/shard_map/ppermute | solution.py:311
  46.2 0.7 collective-permute-done.2.p2
  46.9 2.8 %collective-permute-done.1.p1 = bf16[224,256]{1,0:T(8,128)(2,1)S(1)} collective-permute-done((bf16[224,256]{1,0:T(8,128)(2,1)S(1)}, bf16[224,256]{1,0:T(8,128)(2,1)S(1)}, u32[]{:S(2)}, u32[]{:S(2)}) %collective-permute-start.1) | collective-permute-done | bytes 114720 | tf_op jit(solution)/shard_map/ppermute | solution.py:311
  49.7 0.8 dispatch.1
  50.6 30.2 %all_to_all.16.rows_ref = bf16[32,232,128]{2,1,0:T(8,128)(2,1)S(1)} all-to-all(bf16[32,232,128]{2,1,0:T(8,128)(2,1)S(1)} %get-tuple-element.15), channel_id=1, replica_groups=mesh['ep'=32,'head'=4] {'ep'}, dimensions={0} | all-to-all | bytes 3801088 | tf_op jit(solution)/shard_map/all_to_all | solution.py:347
  80.7 2.1 %expert.1 = bf16[32,224,128]{2,1,0:T(8,128)(2,1)S(1)} custom-call(f32[128,128]{1,0:T(8,128)S(1)} %get-tuple-element.14.slot_weight_ref, bf16[32,232,128]{2,1,0:T(8,128)(2,1)S(1)} %all_to_all.16.rows_ref, bf16[7168,256]{1,0:T(8,128)(2,1)S(1)} %bitcast.16, bf16[7168,256]{1,0:T(8,128)(2,1)S(1)} %bitcast.17, bf16[256,7168]{1,0:T(8,128)(2,1)S(1)} %bitcast.18), custom_call_target="tpu_custom_call" | custom-call | tf_op jit(solution)/shard_map/expert/pallas_call | solution.py:258
  82.8 29.2 %all_to_all.17.returned_ref = bf16[32,224,128]{2,1,0:T(8,128)(2,1)S(1)} all-to-all(bf16[32,224,128]{2,1,0:T(8,128)(2,1)S(1)} %expert.1), channel_id=1, replica_groups=mesh['ep'=32,'head'=4] {'ep'}, dimensions={0} | all-to-all | bytes 3670016 | tf_op jit(solution)/shard_map/all_to_all | solution.py:349
  112.0 0.6 combine.1.c0
  112.6 0.7 collective-permute-start.6
  113.3 0.9 collective-permute-start.4
  114.2 2.6 %collective-permute-done.6.c3 = bf16[224,256]{1,0:T(8,128)(2,1)S(1)} collective-permute-done((bf16[224,256]{1,0:T(8,128)(2,1)S(1)}, bf16[224,256]{1,0:T(8,128)(2,1)S(1)}, u32[]{:S(2)}, u32[]{:S(2)}) %collective-permute-start.6) | collective-permute-done | bytes 114720 | tf_op jit(solution)/shard_map/ppermute | solution.py:311
  116.8 1.8 %collective-permute-done.5.c2 = bf16[224,256]{1,0:T(8,128)(2,1)S(1)} collective-permute-done((bf16[224,256]{1,0:T(8,128)(2,1)S(1)}, bf16[224,256]{1,0:T(8,128)(2,1)S(1)}, u32[]{:S(2)}, u32[]{:S(2)}) %collective-permute-start.5) | collective-permute-done | bytes 114720 | tf_op jit(solution)/shard_map/ppermute | solution.py:311
  118.5 3.7 %collective-permute-done.4.c1 = bf16[224,256]{1,0:T(8,128)(2,1)S(1)} collective-permute-done((bf16[224,256]{1,0:T(8,128)(2,1)S(1)}, bf16[224,256]{1,0:T(8,128)(2,1)S(1)}, u32[]{:S(2)}, u32[]{:S(2)}) %collective-permute-start.4) | collective-permute-done | bytes 114720 | tf_op jit(solution)/shard_map/ppermute | solution.py:311
  122.2 0.9 finish.1
  (18 shorter events, 0.2 us)
Async XLA Ops:
  8.6 33.3 %copy-start.7 = (f32[224]{0:T(256)S(1)}, f32[224]{0:T(256)}, u32[]{:S(2)}) copy-start(f32[224]{0:T(256)} %param.18) | copy-start | bytes 2692
  8.6 33.5 %copy-start.4 = (bf16[256,224]{0,1:T(8,128)(2,1)S(1)}, bf16[256,224]{0,1:T(8,128)(2,1)}, u32[]{:S(2)}) copy-start(bf16[256,224]{0,1:T(8,128)(2,1)} %param.17) | copy-start | bytes 344068
  8.7 33.5 %copy-start.5 = (s32[256,8]{0,1:T(8,128)S(1)}, s32[256,8]{0,1:T(8,128)}, u32[]{:S(2)}) copy-start(s32[256,8]{0,1:T(8,128)} %param.19) | copy-start | bytes 24580
  8.7 33.5 %copy-start.6 = (f32[256,8]{0,1:T(8,128)S(1)}, f32[256,8]{0,1:T(8,128)}, u32[]{:S(2)}) copy-start(f32[256,8]{0,1:T(8,128)} %param.20) | copy-start | bytes 24580
  32.5 4.3 %collective-permute-start = (bf16[128,4096]{1,0:T(8,128)(2,1)S(1)}, bf16[128,4096]{1,0:T(8,128)(2,1)S(1)}, u32[]{:S(2)}, u32[]{:S(2)}) collective-permute-start(bf16[128,4096]{1,0:T(8,128)(2,1)S(1)} %bitcast.14), channel_id=1, source_target_pairs={{0,4},{4,0},{8,12},{12,8},{16,20},{20,16},{24,28},{28,24},{32,36},... | collective-permute-start | bytes 3145736 | tf_op jit(solution)/shard_map/ppermute | solution.py:339
  34.5 1.5 %copy-start = (bf16[4096,224]{0,1:T(8,128)(2,1)S(1)}, bf16[4096,224]{0,1:T(8,128)(2,1)}, u32[]{:S(2)}) copy-start(bf16[4096,224]{0,1:T(8,128)(2,1)} %param.16) | copy-start | bytes 5505028
  37.5 8.8 %collective-permute-start.3 = (bf16[224,256]{1,0:T(8,128)(2,1)S(1)}, bf16[224,256]{1,0:T(8,128)(2,1)S(1)}, u32[]{:S(2)}, u32[]{:S(2)}) collective-permute-start(bf16[224,256]{1,0:T(8,128)(2,1)S(1)} %project.1.p0), channel_id=1, source_target_pairs={{0,3},{1,0},{2,1},{3,2},{4,7},{5,4},{6,5},{7,6},{8,11},{9,8},{10,9... | collective-permute-start | bytes 344072 | tf_op jit(solution)/shard_map/ppermute | solution.py:311
  41.3 5.6 %collective-permute-start.2 = (bf16[224,256]{1,0:T(8,128)(2,1)S(1)}, bf16[224,256]{1,0:T(8,128)(2,1)S(1)}, u32[]{:S(2)}, u32[]{:S(2)}) collective-permute-start(bf16[224,256]{1,0:T(8,128)(2,1)S(1)} %project.1.p0), channel_id=1, source_target_pairs={{0,2},{1,3},{2,0},{3,1},{4,6},{5,7},{6,4},{7,5},{8,10},{9,11},{10,... | collective-permute-start | bytes 344072 | tf_op jit(solution)/shard_map/ppermute | solution.py:311
  41.3 8.4 %collective-permute-start.1 = (bf16[224,256]{1,0:T(8,128)(2,1)S(1)}, bf16[224,256]{1,0:T(8,128)(2,1)S(1)}, u32[]{:S(2)}, u32[]{:S(2)}) collective-permute-start(bf16[224,256]{1,0:T(8,128)(2,1)S(1)} %project.1.p0), channel_id=1, source_target_pairs={{0,1},{1,2},{2,3},{3,0},{4,5},{5,6},{6,7},{7,4},{8,9},{9,10},{10,1... | collective-permute-start | bytes 344072 | tf_op jit(solution)/shard_map/ppermute | solution.py:311
  49.7 31.0 %copy-start.2 = (bf16[1,7168,256]{2,1,0:T(8,128)(2,1)S(1)}, bf16[1,7168,256]{2,1,0:T(8,128)(2,1)}, u32[]{:S(2)}) copy-start(bf16[1,7168,256]{2,1,0:T(8,128)(2,1)} %param.22) | copy-start | bytes 11010052
  49.7 31.0 %copy-start.3 = (bf16[1,256,7168]{2,1,0:T(8,128)(2,1)S(1)}, bf16[1,256,7168]{2,1,0:T(8,128)(2,1)}, u32[]{:S(2)}) copy-start(bf16[1,256,7168]{2,1,0:T(8,128)(2,1)} %param.23) | copy-start | bytes 11010052
  50.5 30.2 %copy-start.1 = (bf16[1,7168,256]{2,1,0:T(8,128)(2,1)S(1)}, bf16[1,7168,256]{2,1,0:T(8,128)(2,1)}, u32[]{:S(2)}) copy-start(bf16[1,7168,256]{2,1,0:T(8,128)(2,1)} %param.21) | copy-start | bytes 11010052
  112.6 4.2 %collective-permute-start.6 = (bf16[224,256]{1,0:T(8,128)(2,1)S(1)}, bf16[224,256]{1,0:T(8,128)(2,1)S(1)}, u32[]{:S(2)}, u32[]{:S(2)}) collective-permute-start(bf16[224,256]{1,0:T(8,128)(2,1)S(1)} %combine.1.c0), channel_id=1, source_target_pairs={{0,3},{1,0},{2,1},{3,2},{4,7},{5,4},{6,5},{7,6},{8,11},{9,8},{10,9... | collective-permute-start | bytes 344072 | tf_op jit(solution)/shard_map/ppermute | solution.py:311
  113.3 5.2 %collective-permute-start.5 = (bf16[224,256]{1,0:T(8,128)(2,1)S(1)}, bf16[224,256]{1,0:T(8,128)(2,1)S(1)}, u32[]{:S(2)}, u32[]{:S(2)}) collective-permute-start(bf16[224,256]{1,0:T(8,128)(2,1)S(1)} %combine.1.c0), channel_id=1, source_target_pairs={{0,2},{1,3},{2,0},{3,1},{4,6},{5,7},{6,4},{7,5},{8,10},{9,11},{10,... | collective-permute-start | bytes 344072 | tf_op jit(solution)/shard_map/ppermute | solution.py:311
  113.3 8.9 %collective-permute-start.4 = (bf16[224,256]{1,0:T(8,128)(2,1)S(1)}, bf16[224,256]{1,0:T(8,128)(2,1)S(1)}, u32[]{:S(2)}, u32[]{:S(2)}) collective-permute-start(bf16[224,256]{1,0:T(8,128)(2,1)S(1)} %combine.1.c0), channel_id=1, source_target_pairs={{0,1},{1,2},{2,3},{3,0},{4,5},{5,6},{6,7},{7,4},{8,9},{9,10},{10,1... | collective-permute-start | bytes 344072 | tf_op jit(solution)/shard_map/ppermute | solution.py:311

commit v5 on v4

--- a/solution.py
+++ b/solution.py
@@ -14,7 +14,7 @@
 SLOTS = 128
 COLS = 224
 ROWS = 232
-GROUP = 4
+GROUP = 8
 TOPK = 8
 PACKED = 16
 SEQS = 4
@@ -59,11 +59,14 @@
     @pl.when(step == pl.num_programs(0) - 1)
     def _():
         up_copy.wait()
-        for h in range(heads):
-            rows = contexts[:, h, :].astype(BF16)
-            values = dot(rows, up_ref[h], NN).astype(BF16)
-            for copy in range(out_ref.shape[0]):
-                out_ref[copy, :, h * width : (h + 1) * width] = values
+        for h in range(0, heads, 2):
+            rows = jnp.concatenate([contexts[:, h, :], contexts[:, h + 1, :]], axis=0).astype(BF16)
+            both = dot(rows, jnp.concatenate([up_ref[h], up_ref[h + 1]], axis=1), NN)
+            seqs = both.shape[0] // 2
+            values = jnp.concatenate([both[:seqs, :width], both[seqs:, width:]], axis=1)
+            values = jnp.concatenate([values, values], axis=0).astype(BF16)
+            for pair in range(out_ref.shape[0]):
+                out_ref[pair, :, h * width : (h + 2) * width] = values
 
 
 def attend(lengths, queries, cache_t, value_up, copies):
@@ -73,14 +76,14 @@
     return pl.pallas_call(
         attend_kernel,
         grid=(seqs // SEQS,),
-        out_shape=jax.ShapeDtypeStruct((copies, seqs, heads * width), BF16),
+        out_shape=jax.ShapeDtypeStruct((copies // 2, 2 * seqs, heads * width), BF16),
         in_specs=[
             pl.BlockSpec(memory_space=pltpu.SMEM),
             pl.BlockSpec((SEQS, heads, kdim), lambda i: (i, 0, 0)),
             pl.BlockSpec((SEQS, kdim, context), lambda i: (i, 0, 0)),
             pl.BlockSpec(memory_space=pl.ANY),
         ],
-        out_specs=pl.BlockSpec((copies, seqs, heads * width), lambda i: (0, 0, 0)),
+        out_specs=pl.BlockSpec((copies // 2, 2 * seqs, heads * width), lambda i: (0, 0, 0)),
         scratch_shapes=[
             pltpu.VMEM((seqs, heads, latent), F32),
             pltpu.VMEM(value_up.shape, BF16),
@@ -90,7 +93,7 @@
         ],
         compiler_params=pltpu.CompilerParams(vmem_limit_bytes=63 * 2**20),
         name="attend",
-    )(lengths, queries, cache_t, value_up)
+    )(lengths, queries, cache_t, value_up).reshape(copies, seqs, heads * width)
 
 
 def slot_onehot(rank_ref, first, count):

time: 123 us -> 123 us (level)
  no operation moved by 1% of the time
where the time goes in v5:
time: 123 us
  blocking collectives  83.2 us (68%)
  waiting for transfers between devices  15.5 us (13%)
  Pallas kernels  14.3 us (12%)
  starting transfers between devices  8.05 us (7%)
  local copies, waits for them, and re-layouts  1.66 us (1%)
    all_to_all x1, blocking collectives, per_device(): lax.all_to_all(outgoing, 'ep', split_axis=0, concat_axis=0, tiled=True)  30.2 us
    all_to_all x1, blocking collectives, per_device(): lax.all_to_all(results, 'ep', split_axis=0, concat_axis=0, tiled=True)  29.2 us
    all_to_all x1, blocking collectives, per_device(): lax.all_to_all(copies, 'ep', split_axis=0, concat_axis=0, tiled=True, axi...  23.9 us
    ppermute x6, waiting for transfers between devices, around_z(): lax.ppermute(part, 'head', [(z, (z + step) % size) for z in range(size)])  15.4 us
    pallas_call x1, Pallas kernels, attend(): pl.pallas_call(attend_kernel, grid=(seqs // SEQS,), out_shape=jax.ShapeDt...  8.46 us
    ppermute x6, starting transfers between devices, around_z(): lax.ppermute(part, 'head', [(z, (z + step) % size) for z in range(size)])  6.07 us
  transfers between devices with their start and end apart: 7, of which 7 were waited for; matrix products, arithmetic and copies ran while one was open for 0% of the time, Pallas kernels for 1%

profile of v5, /device:TPU:1, one launch (start us, length us, event | category | flops | bytes accessed | tf_op | source)
XLA Modules:
  0.0 122.8 jit_solution(736531206713962298)
XLA Ops:
  0.0 8.5 %attend.1 = bf16[8,16,4096]{2,1,0:T(8,128)(2,1)} custom-call(s32[8]{0:T(128)} %lengths_ref.1, bf16[8,32,576]{2,1,0:T(8,128)(2,1)} %queries_ref.1, bf16[8,576,1024]{2,1,0:T(8,128)(2,1)} %bitcast.23, bf16[32,512,128]{2,1,0:T(8,128)(2,1)} %up_hbm.1), custom_call_target="tpu_custom_call" | custom-call | tf_op jit(solution)/shard_map/attend/pallas_call | solution.py:76
  8.5 23.9 %all_to_all.15 = bf16[16,8,4096]{2,1,0:T(8,128)(2,1)S(1)} all-to-all(bf16[16,8,4096]{2,1,0:T(8,128)(2,1)} %bitcast.24), channel_id=1, replica_groups={{0,8,16,24,32,40,48,56,64,72,80,88,96,104,112,120},{4,12,20,28,36,44,52..., dimensions={0} | all-to-all | bytes 2097152 | tf_op jit(solution)/shard_map/all_to_all | solution.py:339
  32.4 2.0 %collective-permute-start = (bf16[128,4096]{1,0:T(8,128)(2,1)S(1)}, bf16[128,4096]{1,0:T(8,128)(2,1)S(1)}, u32[]{:S(2)}, u32[]{:S(2)}) collective-permute-start(bf16[128,4096]{1,0:T(8,128)(2,1)S(1)} %bitcast.15), channel_id=1, source_target_pairs={{0,4},{4,0},{8,12},{12,8},{16,20},{20,16},{24,28},{28,24},{32,36},... | collective-permute-start | bytes 3145736 | tf_op jit(solution)/shard_map/ppermute | solution.py:342
  34.4 1.5 %copy-done = bf16[4096,224]{0,1:T(8,128)(2,1)S(1)} copy-done((bf16[4096,224]{0,1:T(8,128)(2,1)S(1)}, bf16[4096,224]{0,1:T(8,128)(2,1)}, u32[]{:S(2)}) %copy-start) | copy-done | bytes 1835032
  35.9 0.6 project_half.1.first_ref
  36.5 0.1 collective-permute-done.other_ref
  36.6 0.6 project.1.p0
  37.3 3.8 %collective-permute-start.3 = (bf16[224,256]{1,0:T(8,128)(2,1)S(1)}, bf16[224,256]{1,0:T(8,128)(2,1)S(1)}, u32[]{:S(2)}, u32[]{:S(2)}) collective-permute-start(bf16[224,256]{1,0:T(8,128)(2,1)S(1)} %project.1.p0), channel_id=1, source_target_pairs={{0,3},{1,0},{2,1},{3,2},{4,7},{5,4},{6,5},{7,6},{8,11},{9,8},{10,9... | collective-permute-start | bytes 344072 | tf_op jit(solution)/shard_map/ppermute | solution.py:314
  41.1 0.7 collective-permute-start.1
  42.0 0.3 route.1
  42.3 3.8 %collective-permute-done.3.p3 = bf16[224,256]{1,0:T(8,128)(2,1)S(1)} collective-permute-done((bf16[224,256]{1,0:T(8,128)(2,1)S(1)}, bf16[224,256]{1,0:T(8,128)(2,1)S(1)}, u32[]{:S(2)}, u32[]{:S(2)}) %collective-permute-start.3) | collective-permute-done | bytes 114720 | tf_op jit(solution)/shard_map/ppermute | solution.py:314
  46.0 0.7 collective-permute-done.2.p2
  46.7 2.8 %collective-permute-done.1.p1 = bf16[224,256]{1,0:T(8,128)(2,1)S(1)} collective-permute-done((bf16[224,256]{1,0:T(8,128)(2,1)S(1)}, bf16[224,256]{1,0:T(8,128)(2,1)S(1)}, u32[]{:S(2)}, u32[]{:S(2)}) %collective-permute-start.1) | collective-permute-done | bytes 114720 | tf_op jit(solution)/shard_map/ppermute | solution.py:314
  49.5 0.8 dispatch.1
  50.4 30.2 %all_to_all.16.rows_ref = bf16[32,232,128]{2,1,0:T(8,128)(2,1)S(1)} all-to-all(bf16[32,232,128]{2,1,0:T(8,128)(2,1)S(1)} %get-tuple-element.15), channel_id=1, replica_groups=mesh['ep'=32,'head'=4] {'ep'}, dimensions={0} | all-to-all | bytes 3801088 | tf_op jit(solution)/shard_map/all_to_all | solution.py:350
  80.6 1.9 %expert.1 = bf16[32,224,128]{2,1,0:T(8,128)(2,1)S(1)} custom-call(f32[128,128]{1,0:T(8,128)S(1)} %get-tuple-element.14.slot_weight_ref, bf16[32,232,128]{2,1,0:T(8,128)(2,1)S(1)} %all_to_all.16.rows_ref, bf16[7168,256]{1,0:T(8,128)(2,1)S(1)} %bitcast.17, bf16[7168,256]{1,0:T(8,128)(2,1)S(1)} %bitcast.18, bf16[256,7168]{1,0:T(8,128)(2,1)S(1)} %bitcast.19), custom_call_target="tpu_custom_call" | custom-call | tf_op jit(solution)/shard_map/expert/pallas_call | solution.py:261
  82.5 29.2 %all_to_all.17.returned_ref = bf16[32,224,128]{2,1,0:T(8,128)(2,1)S(1)} all-to-all(bf16[32,224,128]{2,1,0:T(8,128)(2,1)S(1)} %expert.1), channel_id=1, replica_groups=mesh['ep'=32,'head'=4] {'ep'}, dimensions={0} | all-to-all | bytes 3670016 | tf_op jit(solution)/shard_map/all_to_all | solution.py:352
  111.7 0.6 combine.1.c0
  112.3 0.7 collective-permute-start.6
  113.0 0.8 collective-permute-start.4
  113.8 2.6 %collective-permute-done.6.c3 = bf16[224,256]{1,0:T(8,128)(2,1)S(1)} collective-permute-done((bf16[224,256]{1,0:T(8,128)(2,1)S(1)}, bf16[224,256]{1,0:T(8,128)(2,1)S(1)}, u32[]{:S(2)}, u32[]{:S(2)}) %collective-permute-start.6) | collective-permute-done | bytes 114720 | tf_op jit(solution)/shard_map/ppermute | solution.py:314
  116.5 1.8 %collective-permute-done.5.c2 = bf16[224,256]{1,0:T(8,128)(2,1)S(1)} collective-permute-done((bf16[224,256]{1,0:T(8,128)(2,1)S(1)}, bf16[224,256]{1,0:T(8,128)(2,1)S(1)}, u32[]{:S(2)}, u32[]{:S(2)}) %collective-permute-start.5) | collective-permute-done | bytes 114720 | tf_op jit(solution)/shard_map/ppermute | solution.py:314
  118.2 3.7 %collective-permute-done.4.c1 = bf16[224,256]{1,0:T(8,128)(2,1)S(1)} collective-permute-done((bf16[224,256]{1,0:T(8,128)(2,1)S(1)}, bf16[224,256]{1,0:T(8,128)(2,1)S(1)}, u32[]{:S(2)}, u32[]{:S(2)}) %collective-permute-start.4) | collective-permute-done | bytes 114720 | tf_op jit(solution)/shard_map/ppermute | solution.py:314
  121.9 0.9 finish.1
  (18 shorter events, 0.2 us)
Async XLA Ops:
  8.5 33.3 %copy-start.7 = (f32[224]{0:T(256)S(1)}, f32[224]{0:T(256)}, u32[]{:S(2)}) copy-start(f32[224]{0:T(256)} %param.18) | copy-start | bytes 2692
  8.5 33.5 %copy-start.4 = (bf16[256,224]{0,1:T(8,128)(2,1)S(1)}, bf16[256,224]{0,1:T(8,128)(2,1)}, u32[]{:S(2)}) copy-start(bf16[256,224]{0,1:T(8,128)(2,1)} %param.17) | copy-start | bytes 344068
  8.5 33.5 %copy-start.5 = (s32[256,8]{0,1:T(8,128)S(1)}, s32[256,8]{0,1:T(8,128)}, u32[]{:S(2)}) copy-start(s32[256,8]{0,1:T(8,128)} %param.19) | copy-start | bytes 24580
  8.5 33.5 %copy-start.6 = (f32[256,8]{0,1:T(8,128)S(1)}, f32[256,8]{0,1:T(8,128)}, u32[]{:S(2)}) copy-start(f32[256,8]{0,1:T(8,128)} %param.20) | copy-start | bytes 24580
  32.4 4.3 %collective-permute-start = (bf16[128,4096]{1,0:T(8,128)(2,1)S(1)}, bf16[128,4096]{1,0:T(8,128)(2,1)S(1)}, u32[]{:S(2)}, u32[]{:S(2)}) collective-permute-start(bf16[128,4096]{1,0:T(8,128)(2,1)S(1)} %bitcast.15), channel_id=1, source_target_pairs={{0,4},{4,0},{8,12},{12,8},{16,20},{20,16},{24,28},{28,24},{32,36},... | collective-permute-start | bytes 3145736 | tf_op jit(solution)/shard_map/ppermute | solution.py:342
  34.4 1.5 %copy-start = (bf16[4096,224]{0,1:T(8,128)(2,1)S(1)}, bf16[4096,224]{0,1:T(8,128)(2,1)}, u32[]{:S(2)}) copy-start(bf16[4096,224]{0,1:T(8,128)(2,1)} %param.16) | copy-start | bytes 5505028
  37.3 8.8 %collective-permute-start.3 = (bf16[224,256]{1,0:T(8,128)(2,1)S(1)}, bf16[224,256]{1,0:T(8,128)(2,1)S(1)}, u32[]{:S(2)}, u32[]{:S(2)}) collective-permute-start(bf16[224,256]{1,0:T(8,128)(2,1)S(1)} %project.1.p0), channel_id=1, source_target_pairs={{0,3},{1,0},{2,1},{3,2},{4,7},{5,4},{6,5},{7,6},{8,11},{9,8},{10,9... | collective-permute-start | bytes 344072 | tf_op jit(solution)/shard_map/ppermute | solution.py:314
  41.1 5.6 %collective-permute-start.2 = (bf16[224,256]{1,0:T(8,128)(2,1)S(1)}, bf16[224,256]{1,0:T(8,128)(2,1)S(1)}, u32[]{:S(2)}, u32[]{:S(2)}) collective-permute-start(bf16[224,256]{1,0:T(8,128)(2,1)S(1)} %project.1.p0), channel_id=1, source_target_pairs={{0,2},{1,3},{2,0},{3,1},{4,6},{5,7},{6,4},{7,5},{8,10},{9,11},{10,... | collective-permute-start | bytes 344072 | tf_op jit(solution)/shard_map/ppermute | solution.py:314
  41.1 8.4 %collective-permute-start.1 = (bf16[224,256]{1,0:T(8,128)(2,1)S(1)}, bf16[224,256]{1,0:T(8,128)(2,1)S(1)}, u32[]{:S(2)}, u32[]{:S(2)}) collective-permute-start(bf16[224,256]{1,0:T(8,128)(2,1)S(1)} %project.1.p0), channel_id=1, source_target_pairs={{0,1},{1,2},{2,3},{3,0},{4,5},{5,6},{6,7},{7,4},{8,9},{9,10},{10,1... | collective-permute-start | bytes 344072 | tf_op jit(solution)/shard_map/ppermute | solution.py:314
  49.5 31.0 %copy-start.2 = (bf16[1,7168,256]{2,1,0:T(8,128)(2,1)S(1)}, bf16[1,7168,256]{2,1,0:T(8,128)(2,1)}, u32[]{:S(2)}) copy-start(bf16[1,7168,256]{2,1,0:T(8,128)(2,1)} %param.22) | copy-start | bytes 11010052
  49.5 31.0 %copy-start.3 = (bf16[1,256,7168]{2,1,0:T(8,128)(2,1)S(1)}, bf16[1,256,7168]{2,1,0:T(8,128)(2,1)}, u32[]{:S(2)}) copy-start(bf16[1,256,7168]{2,1,0:T(8,128)(2,1)} %param.23) | copy-start | bytes 11010052
  50.4 30.2 %copy-start.1 = (bf16[1,7168,256]{2,1,0:T(8,128)(2,1)S(1)}, bf16[1,7168,256]{2,1,0:T(8,128)(2,1)}, u32[]{:S(2)}) copy-start(bf16[1,7168,256]{2,1,0:T(8,128)(2,1)} %param.21) | copy-start | bytes 11010052
  112.3 4.2 %collective-permute-start.6 = (bf16[224,256]{1,0:T(8,128)(2,1)S(1)}, bf16[224,256]{1,0:T(8,128)(2,1)S(1)}, u32[]{:S(2)}, u32[]{:S(2)}) collective-permute-start(bf16[224,256]{1,0:T(8,128)(2,1)S(1)} %combine.1.c0), channel_id=1, source_target_pairs={{0,3},{1,0},{2,1},{3,2},{4,7},{5,4},{6,5},{7,6},{8,11},{9,8},{10,9... | collective-permute-start | bytes 344072 | tf_op jit(solution)/shard_map/ppermute | solution.py:314
  113.0 5.3 %collective-permute-start.5 = (bf16[224,256]{1,0:T(8,128)(2,1)S(1)}, bf16[224,256]{1,0:T(8,128)(2,1)S(1)}, u32[]{:S(2)}, u32[]{:S(2)}) collective-permute-start(bf16[224,256]{1,0:T(8,128)(2,1)S(1)} %combine.1.c0), channel_id=1, source_target_pairs={{0,2},{1,3},{2,0},{3,1},{4,6},{5,7},{6,4},{7,5},{8,10},{9,11},{10,... | collective-permute-start | bytes 344072 | tf_op jit(solution)/shard_map/ppermute | solution.py:314
  113.0 8.9 %collective-permute-start.4 = (bf16[224,256]{1,0:T(8,128)(2,1)S(1)}, bf16[224,256]{1,0:T(8,128)(2,1)S(1)}, u32[]{:S(2)}, u32[]{:S(2)}) collective-permute-start(bf16[224,256]{1,0:T(8,128)(2,1)S(1)} %combine.1.c0), channel_id=1, source_target_pairs={{0,1},{1,2},{2,3},{3,0},{4,5},{5,6},{6,7},{7,4},{8,9},{9,10},{10,1... | collective-permute-start | bytes 344072 | tf_op jit(solution)/shard_map/ppermute | solution.py:314

commit v6 on v5

--- a/solution.py
+++ b/solution.py
@@ -32,11 +32,12 @@
 
 
 def attend_kernel(
-    lengths_ref, queries_ref, cache_ref, up_hbm, out_ref, contexts, up_ref, scores, probs, up_sem
+    lengths_ref, queries_ref, *refs
 ):
+    caches, (up_hbm, out_ref, contexts, up_ref, scores, probs, up_sem) = refs[:SEQS], refs[SEQS:]
     step = pl.program_id(0)
     heads, latent, width = up_ref.shape
-    context = cache_ref.shape[2]
+    context = caches[0].shape[2]
     up_copy = pltpu.make_async_copy(up_hbm, up_ref, up_sem)
 
     @pl.when(step == 0)
@@ -44,7 +45,7 @@
         up_copy.start()
 
     for b in range(SEQS):
-        scores[b] = dot(queries_ref[b], cache_ref[b], NN)
+        scores[b] = dot(queries_ref[b], caches[b][0], NN)
     for b in range(SEQS):
         seq = step * SEQS + b
         positions = lax.broadcasted_iota(jnp.int32, (PACKED, context), 1)
@@ -54,7 +55,7 @@
             exponents = jnp.exp(part - jnp.max(part, axis=1, keepdims=True))
             total = jnp.sum(exponents, axis=1, keepdims=True)
             probs[b, r : r + PACKED] = (exponents / total).astype(BF16)
-        contexts[seq] = dot(probs[b], cache_ref[b, :latent, :], NT)
+        contexts[seq] = dot(probs[b], caches[b][0, :latent, :], NT)
 
     @pl.when(step == pl.num_programs(0) - 1)
     def _():
@@ -80,7 +81,10 @@
         in_specs=[
             pl.BlockSpec(memory_space=pltpu.SMEM),
             pl.BlockSpec((SEQS, heads, kdim), lambda i: (i, 0, 0)),
-            pl.BlockSpec((SEQS, kdim, context), lambda i: (i, 0, 0)),
+            *(
+                pl.BlockSpec((1, kdim, context), lambda i, b=b: (i * SEQS + b, 0, 0))
+                for b in range(SEQS)
+            ),
             pl.BlockSpec(memory_space=pl.ANY),
         ],
         out_specs=pl.BlockSpec((copies // 2, 2 * seqs, heads * width), lambda i: (0, 0, 0)),
@@ -91,9 +95,9 @@
             pltpu.VMEM((SEQS, heads, context), BF16),
             pltpu.SemaphoreType.DMA,
         ],
-        compiler_params=pltpu.CompilerParams(vmem_limit_bytes=63 * 2**20),
+        compiler_params=pltpu.CompilerParams(vmem_limit_bytes=61 * 2**20),
         name="attend",
-    )(lengths, queries, cache_t, value_up).reshape(copies, seqs, heads * width)
+    )(lengths, queries, *[cache_t] * SEQS, value_up).reshape(copies, seqs, heads * width)
 
 
 def slot_onehot(rank_ref, first, count):

time: 123 us -> 123 us (level)
  waiting for transfers between devices: 15.5 us -> 17 us
  local copies, waits for them, and re-layouts: 1.66 us -> 0.17 us
    ppermute x1, waiting for transfers between devices: 0.15 us -> 1.64 us  [per_device(): other = lax.ppermute(mine, 'ep', [(i, i ^ 1) for i in range(EXPERTS)])]
    unnamed x16, local copies, waits for them, and re-layouts: 1.54 us -> 0.04 us
where the time goes in v6:
time: 123 us
  blocking collectives  83.2 us (68%)
  waiting for transfers between devices  17 us (14%)
  Pallas kernels  14.4 us (12%)
  starting transfers between devices  8.04 us (7%)
    all_to_all x1, blocking collectives, per_device(): lax.all_to_all(outgoing, 'ep', split_axis=0, concat_axis=0, tiled=True)  30.2 us
    all_to_all x1, blocking collectives, per_device(): lax.all_to_all(results, 'ep', split_axis=0, concat_axis=0, tiled=True)  29.2 us
    all_to_all x1, blocking collectives, per_device(): lax.all_to_all(copies, 'ep', split_axis=0, concat_axis=0, tiled=True, axi...  23.9 us
    ppermute x6, waiting for transfers between devices, around_z(): lax.ppermute(part, 'head', [(z, (z + step) % size) for z in range(size)])  15.4 us
    pallas_call x1, Pallas kernels, attend(): pl.pallas_call(attend_kernel, grid=(seqs // SEQS,), out_shape=jax.ShapeDt...  8.56 us
    ppermute x6, starting transfers between devices, around_z(): lax.ppermute(part, 'head', [(z, (z + step) % size) for z in range(size)])  6.06 us
  transfers between devices with their start and end apart: 7, of which 7 were waited for; matrix products, arithmetic and copies ran while one was open for 0% of the time, Pallas kernels for 1%

profile of v6, /device:TPU:1, one launch (start us, length us, event | category | flops | bytes accessed | tf_op | source)
XLA Modules:
  0.0 122.9 jit_solution(10385346188606185783)
XLA Ops:
  0.0 8.6 %attend.1 = bf16[8,16,4096]{2,1,0:T(8,128)(2,1)} custom-call(s32[8]{0:T(128)} %lengths_ref.1, bf16[8,32,576]{2,1,0:T(8,128)(2,1)} %queries_ref.1, bf16[8,576,1024]{2,1,0:T(8,128)(2,1)} %bitcast.23, bf16[8,576,1024]{2,1,0:T(8,128)(2,1)} %bitcast.24, bf16[8,576,1024]{2,1,0:T(8,128)(2,1)} %bitcast.25, bf16[8,576,1024]{2,1,0:T(8,128)(2,1)} %bitcast.26, ...), custom_call_target="tpu_custom_call" | custom-call | tf_op jit(solution)/shard_map/attend/pallas_call | solution.py:77
  8.6 23.9 %all_to_all.15 = bf16[16,8,4096]{2,1,0:T(8,128)(2,1)S(1)} all-to-all(bf16[16,8,4096]{2,1,0:T(8,128)(2,1)} %bitcast.27), channel_id=1, replica_groups={{0,8,16,24,32,40,48,56,64,72,80,88,96,104,112,120},{4,12,20,28,36,44,52..., dimensions={0} | all-to-all | bytes 2097152 | tf_op jit(solution)/shard_map/all_to_all | solution.py:343
  32.5 2.0 %collective-permute-start = (bf16[128,4096]{1,0:T(8,128)(2,1)S(1)}, bf16[128,4096]{1,0:T(8,128)(2,1)S(1)}, u32[]{:S(2)}, u32[]{:S(2)}) collective-permute-start(bf16[128,4096]{1,0:T(8,128)(2,1)S(1)} %bitcast.15), channel_id=1, source_target_pairs={{0,4},{4,0},{8,12},{12,8},{16,20},{20,16},{24,28},{28,24},{32,36},... | collective-permute-start | bytes 3145736 | tf_op jit(solution)/shard_map/ppermute | solution.py:346
  34.5 0.6 project_half.1.first_ref
  35.1 1.6 %collective-permute-done.other_ref = bf16[128,4096]{1,0:T(8,128)(2,1)S(1)} collective-permute-done((bf16[128,4096]{1,0:T(8,128)(2,1)S(1)}, bf16[128,4096]{1,0:T(8,128)(2,1)S(1)}, u32[]{:S(2)}, u32[]{:S(2)}) %collective-permute-start) | collective-permute-done | bytes 1048608 | tf_op jit(solution)/shard_map/ppermute | solution.py:346
  36.7 0.6 project.1.p0
  37.4 3.8 %collective-permute-start.3 = (bf16[224,256]{1,0:T(8,128)(2,1)S(1)}, bf16[224,256]{1,0:T(8,128)(2,1)S(1)}, u32[]{:S(2)}, u32[]{:S(2)}) collective-permute-start(bf16[224,256]{1,0:T(8,128)(2,1)S(1)} %project.1.p0), channel_id=1, source_target_pairs={{0,3},{1,0},{2,1},{3,2},{4,7},{5,4},{6,5},{7,6},{8,11},{9,8},{10,9... | collective-permute-start | bytes 344072 | tf_op jit(solution)/shard_map/ppermute | solution.py:318
  41.2 0.7 collective-permute-start.1
  41.9 0.1 copy.13.gain_ref
  42.1 0.3 route.1
  42.3 3.8 %collective-permute-done.3.p3 = bf16[224,256]{1,0:T(8,128)(2,1)S(1)} collective-permute-done((bf16[224,256]{1,0:T(8,128)(2,1)S(1)}, bf16[224,256]{1,0:T(8,128)(2,1)S(1)}, u32[]{:S(2)}, u32[]{:S(2)}) %collective-permute-start.3) | collective-permute-done | bytes 114720 | tf_op jit(solution)/shard_map/ppermute | solution.py:318
  46.1 0.7 collective-permute-done.2.p2
  46.8 2.8 %collective-permute-done.1.p1 = bf16[224,256]{1,0:T(8,128)(2,1)S(1)} collective-permute-done((bf16[224,256]{1,0:T(8,128)(2,1)S(1)}, bf16[224,256]{1,0:T(8,128)(2,1)S(1)}, u32[]{:S(2)}, u32[]{:S(2)}) %collective-permute-start.1) | collective-permute-done | bytes 114720 | tf_op jit(solution)/shard_map/ppermute | solution.py:318
  49.7 0.8 dispatch.1
  50.5 30.2 %all_to_all.16.rows_ref = bf16[32,232,128]{2,1,0:T(8,128)(2,1)S(1)} all-to-all(bf16[32,232,128]{2,1,0:T(8,128)(2,1)S(1)} %get-tuple-element.15), channel_id=1, replica_groups=mesh['ep'=32,'head'=4] {'ep'}, dimensions={0} | all-to-all | bytes 3801088 | tf_op jit(solution)/shard_map/all_to_all | solution.py:354
  80.7 1.9 %expert.1 = bf16[32,224,128]{2,1,0:T(8,128)(2,1)S(1)} custom-call(f32[128,128]{1,0:T(8,128)S(1)} %get-tuple-element.14.slot_weight_ref, bf16[32,232,128]{2,1,0:T(8,128)(2,1)S(1)} %all_to_all.16.rows_ref, bf16[7168,256]{1,0:T(8,128)(2,1)S(1)} %bitcast.17, bf16[7168,256]{1,0:T(8,128)(2,1)S(1)} %bitcast.18, bf16[256,7168]{1,0:T(8,128)(2,1)S(1)} %bitcast.19), custom_call_target="tpu_custom_call" | custom-call | tf_op jit(solution)/shard_map/expert/pallas_call | solution.py:265
  82.6 29.2 %all_to_all.17.returned_ref = bf16[32,224,128]{2,1,0:T(8,128)(2,1)S(1)} all-to-all(bf16[32,224,128]{2,1,0:T(8,128)(2,1)S(1)} %expert.1), channel_id=1, replica_groups=mesh['ep'=32,'head'=4] {'ep'}, dimensions={0} | all-to-all | bytes 3670016 | tf_op jit(solution)/shard_map/all_to_all | solution.py:356
  111.8 0.6 combine.1.c0
  112.4 0.7 collective-permute-start.6
  113.1 0.8 collective-permute-start.4
  114.0 2.6 %collective-permute-done.6.c3 = bf16[224,256]{1,0:T(8,128)(2,1)S(1)} collective-permute-done((bf16[224,256]{1,0:T(8,128)(2,1)S(1)}, bf16[224,256]{1,0:T(8,128)(2,1)S(1)}, u32[]{:S(2)}, u32[]{:S(2)}) %collective-permute-start.6) | collective-permute-done | bytes 114720 | tf_op jit(solution)/shard_map/ppermute | solution.py:318
  116.6 1.8 %collective-permute-done.5.c2 = bf16[224,256]{1,0:T(8,128)(2,1)S(1)} collective-permute-done((bf16[224,256]{1,0:T(8,128)(2,1)S(1)}, bf16[224,256]{1,0:T(8,128)(2,1)S(1)}, u32[]{:S(2)}, u32[]{:S(2)}) %collective-permute-start.5) | collective-permute-done | bytes 114720 | tf_op jit(solution)/shard_map/ppermute | solution.py:318
  118.4 3.7 %collective-permute-done.4.c1 = bf16[224,256]{1,0:T(8,128)(2,1)S(1)} collective-permute-done((bf16[224,256]{1,0:T(8,128)(2,1)S(1)}, bf16[224,256]{1,0:T(8,128)(2,1)S(1)}, u32[]{:S(2)}, u32[]{:S(2)}) %collective-permute-start.4) | collective-permute-done | bytes 114720 | tf_op jit(solution)/shard_map/ppermute | solution.py:318
  122.0 0.9 finish.1
  (18 shorter events, 0.0 us)
Async XLA Ops:
  0.0 34.5 %copy-start = (bf16[4096,224]{0,1:T(8,128)(2,1)S(1)}, bf16[4096,224]{0,1:T(8,128)(2,1)}, u32[]{:S(2)}) copy-start(bf16[4096,224]{0,1:T(8,128)(2,1)} %param.16) | copy-start | bytes 5505028
  8.6 33.3 %copy-start.7 = (f32[224]{0:T(256)S(1)}, f32[224]{0:T(256)}, u32[]{:S(2)}) copy-start(f32[224]{0:T(256)} %param.18) | copy-start | bytes 2692
  8.6 33.5 %copy-start.4 = (bf16[256,224]{0,1:T(8,128)(2,1)S(1)}, bf16[256,224]{0,1:T(8,128)(2,1)}, u32[]{:S(2)}) copy-start(bf16[256,224]{0,1:T(8,128)(2,1)} %param.17) | copy-start | bytes 344068
  8.6 33.5 %copy-start.5 = (s32[256,8]{0,1:T(8,128)S(1)}, s32[256,8]{0,1:T(8,128)}, u32[]{:S(2)}) copy-start(s32[256,8]{0,1:T(8,128)} %param.19) | copy-start | bytes 24580
  8.6 33.5 %copy-start.6 = (f32[256,8]{0,1:T(8,128)S(1)}, f32[256,8]{0,1:T(8,128)}, u32[]{:S(2)}) copy-start(f32[256,8]{0,1:T(8,128)} %param.20) | copy-start | bytes 24580
  32.5 4.3 %collective-permute-start = (bf16[128,4096]{1,0:T(8,128)(2,1)S(1)}, bf16[128,4096]{1,0:T(8,128)(2,1)S(1)}, u32[]{:S(2)}, u32[]{:S(2)}) collective-permute-start(bf16[128,4096]{1,0:T(8,128)(2,1)S(1)} %bitcast.15), channel_id=1, source_target_pairs={{0,4},{4,0},{8,12},{12,8},{16,20},{20,16},{24,28},{28,24},{32,36},... | collective-permute-start | bytes 3145736 | tf_op jit(solution)/shard_map/ppermute | solution.py:346
  37.4 8.8 %collective-permute-start.3 = (bf16[224,256]{1,0:T(8,128)(2,1)S(1)}, bf16[224,256]{1,0:T(8,128)(2,1)S(1)}, u32[]{:S(2)}, u32[]{:S(2)}) collective-permute-start(bf16[224,256]{1,0:T(8,128)(2,1)S(1)} %project.1.p0), channel_id=1, source_target_pairs={{0,3},{1,0},{2,1},{3,2},{4,7},{5,4},{6,5},{7,6},{8,11},{9,8},{10,9... | collective-permute-start | bytes 344072 | tf_op jit(solution)/shard_map/ppermute | solution.py:318
  41.2 5.6 %collective-permute-start.2 = (bf16[224,256]{1,0:T(8,128)(2,1)S(1)}, bf16[224,256]{1,0:T(8,128)(2,1)S(1)}, u32[]{:S(2)}, u32[]{:S(2)}) collective-permute-start(bf16[224,256]{1,0:T(8,128)(2,1)S(1)} %project.1.p0), channel_id=1, source_target_pairs={{0,2},{1,3},{2,0},{3,1},{4,6},{5,7},{6,4},{7,5},{8,10},{9,11},{10,... | collective-permute-start | bytes 344072 | tf_op jit(solution)/shard_map/ppermute | solution.py:318
  41.2 8.4 %collective-permute-start.1 = (bf16[224,256]{1,0:T(8,128)(2,1)S(1)}, bf16[224,256]{1,0:T(8,128)(2,1)S(1)}, u32[]{:S(2)}, u32[]{:S(2)}) collective-permute-start(bf16[224,256]{1,0:T(8,128)(2,1)S(1)} %project.1.p0), channel_id=1, source_target_pairs={{0,1},{1,2},{2,3},{3,0},{4,5},{5,6},{6,7},{7,4},{8,9},{9,10},{10,1... | collective-permute-start | bytes 344072 | tf_op jit(solution)/shard_map/ppermute | solution.py:318
  49.6 31.0 %copy-start.2 = (bf16[1,7168,256]{2,1,0:T(8,128)(2,1)S(1)}, bf16[1,7168,256]{2,1,0:T(8,128)(2,1)}, u32[]{:S(2)}) copy-start(bf16[1,7168,256]{2,1,0:T(8,128)(2,1)} %param.22) | copy-start | bytes 11010052
  49.6 31.0 %copy-start.3 = (bf16[1,256,7168]{2,1,0:T(8,128)(2,1)S(1)}, bf16[1,256,7168]{2,1,0:T(8,128)(2,1)}, u32[]{:S(2)}) copy-start(bf16[1,256,7168]{2,1,0:T(8,128)(2,1)} %param.23) | copy-start | bytes 11010052
  50.5 30.2 %copy-start.1 = (bf16[1,7168,256]{2,1,0:T(8,128)(2,1)S(1)}, bf16[1,7168,256]{2,1,0:T(8,128)(2,1)}, u32[]{:S(2)}) copy-start(bf16[1,7168,256]{2,1,0:T(8,128)(2,1)} %param.21) | copy-start | bytes 11010052
  112.4 4.2 %collective-permute-start.6 = (bf16[224,256]{1,0:T(8,128)(2,1)S(1)}, bf16[224,256]{1,0:T(8,128)(2,1)S(1)}, u32[]{:S(2)}, u32[]{:S(2)}) collective-permute-start(bf16[224,256]{1,0:T(8,128)(2,1)S(1)} %combine.1.c0), channel_id=1, source_target_pairs={{0,3},{1,0},{2,1},{3,2},{4,7},{5,4},{6,5},{7,6},{8,11},{9,8},{10,9... | collective-permute-start | bytes 344072 | tf_op jit(solution)/shard_map/ppermute | solution.py:318
  113.1 5.3 %collective-permute-start.5 = (bf16[224,256]{1,0:T(8,128)(2,1)S(1)}, bf16[224,256]{1,0:T(8,128)(2,1)S(1)}, u32[]{:S(2)}, u32[]{:S(2)}) collective-permute-start(bf16[224,256]{1,0:T(8,128)(2,1)S(1)} %combine.1.c0), channel_id=1, source_target_pairs={{0,2},{1,3},{2,0},{3,1},{4,6},{5,7},{6,4},{7,5},{8,10},{9,11},{10,... | collective-permute-start | bytes 344072 | tf_op jit(solution)/shard_map/ppermute | solution.py:318
  113.1 8.9 %collective-permute-start.4 = (bf16[224,256]{1,0:T(8,128)(2,1)S(1)}, bf16[224,256]{1,0:T(8,128)(2,1)S(1)}, u32[]{:S(2)}, u32[]{:S(2)}) collective-permute-start(bf16[224,256]{1,0:T(8,128)(2,1)S(1)} %combine.1.c0), channel_id=1, source_target_pairs={{0,1},{1,2},{2,3},{3,0},{4,5},{5,6},{6,7},{7,4},{8,9},{9,10},{10,1... | collective-permute-start | bytes 344072 | tf_op jit(solution)/shard_map/ppermute | solution.py:318
